TPU v7x, 256 devices: a whole 4x4x8 slice. The times are simulated.
256 devices in a mesh: row: 16 (over x, z_hi), col: 16 (over y, z_lo, core).
Axes of the slice: x: 4, y: 4, z: 8 (z_hi: 4, z_lo: 2; z = z_hi * 2 + z_lo), core: 2. Of those that a mesh axis runs over, the one named last changes fastest.
Arguments:
- image_feats: bfloat16 [32768, 1408], P(('row', 'col')), may hold values from -6 to 6
- text_emb: bfloat16 [32768, 1024], P(('row', 'col')), may hold values from -6 to 6
- projection: bfloat16 [1408, 1024], replicated, may hold values from -0.15625 to 0.15625
- clip_norms: float32 [4096], P(('row', 'col')), may hold values from 10 to 200
- user_ids: int32 [32768], P(('row', 'col')), may hold values from 0 to 4095, as said below
- grad_sum: float32 [11264, 128], P(('row', 'col')), may hold values from -8 to 8
- init_weights: float32 [11264, 128], P(('row', 'col')), may hold values from -0.15625 to 0.15625
- tree_noise: float32 [11264, 128], P(('row', 'col')), may hold values from -20 to 20
Outputs:
- new_weights: bfloat16 [1408, 1024], replicated
- new_grad_sum: float32 [11264, 128], P(('row', 'col'))
Inputs may be any that keep to these rules, and one draw needn't show every extreme that they name: `user_ids`: the pairs of rows b * 128 to (b + 1) * 128 - 1 (the pairs of one device) carry the user ids b * 16 to (b + 1) * 16 - 1, each at least once, so all pairs of a user lie in one such block.
All inputs are finite; a program needn't handle non-finite values.
Results may differ from a plain program's by a relative error of at most 0.0049.
The roundings to bfloat16 on the way count: a program that leaves them out, or rounds other values in their place, can miss the bound.
Values may be sent and summed in bfloat16 or wider, within the bound.
A program may use at most 64 MiB of HBM per device.

v0:
```python
import math

import jax
import jax.numpy as jnp
from jax import lax
from jax.sharding import PartitionSpec as P

LOGIT_SCALE = 32.0
LOGIT_BIAS = -5.0
RATE = 0.5
EPSILON = 1e-06


def make_fold(text_block, image_offset, text_offset, own_pairs):

    def fold_rows(running, shard_rows, first_row):
        row_count = shard_rows.shape[0]
        logits = (
            LOGIT_SCALE
            * lax.dot_general(
                shard_rows, text_block, (((1,), (1,)), ((), ())), preferred_element_type=jnp.float32
            )
            + LOGIT_BIAS
        )
        local_row = lax.broadcasted_iota(jnp.int32, (row_count, 1), 0) - image_offset
        text_index = lax.broadcasted_iota(jnp.int32, (1, text_block.shape[0]), 1)
        positive = (
            (text_index == local_row + text_offset) & (local_row >= 0) & (local_row < own_pairs)
        ).astype(jnp.float32)
        pair_weight = (jax.nn.sigmoid(logits) - positive).astype(jnp.bfloat16)
        row_grads = LOGIT_SCALE * jnp.dot(
            pair_weight, text_block, preferred_element_type=jnp.float32
        )
        return row_grads

    return fold_rows


def body(
    image_feats, text_emb, projection, clip_norms, user_ids, grad_sum, init_weights, tree_noise
):
    own_pairs = image_feats.shape[0]
    embed_width = projection.shape[1]
    image_raw = jnp.dot(image_feats, projection, preferred_element_type=jnp.float32)
    inverse = lax.rsqrt(jnp.sum(image_raw * image_raw, axis=1, keepdims=True) + EPSILON)
    image_unit = (image_raw * inverse).astype(jnp.bfloat16)
    text_float = text_emb.astype(jnp.float32)
    text_unit = (
        text_float * lax.rsqrt(jnp.sum(text_float * text_float, axis=1, keepdims=True) + EPSILON)
    ).astype(jnp.bfloat16)
    row_index = lax.axis_index("row")
    col_index = lax.axis_index("col")
    text_block = lax.all_gather(text_unit, "row", axis=0, tiled=True)
    folder = make_fold(text_block, col_index * own_pairs, row_index * own_pairs, own_pairs)
    empty = jnp.zeros((lax.axis_size("col") * own_pairs, embed_width), jnp.float32)
    partial_value = folder(
        empty, lax.all_gather(image_unit, "col", axis=0, tiled=True), jnp.int32(0)
    )
    unit_grad = lax.psum_scatter(partial_value, "col", scatter_dimension=0, tiled=True)
    inner = jnp.sum(image_raw * unit_grad, axis=1, keepdims=True)
    embed_grad = inverse * unit_grad - inverse * inverse * inverse * image_raw * inner
    feat_gram = lax.dot_general(
        image_feats, image_feats, (((1,), (1,)), ((), ())), preferred_element_type=jnp.float32
    )
    grad_gram = lax.dot_general(
        embed_grad, embed_grad, (((1,), (1,)), ((), ())), precision=lax.Precision.HIGHEST
    )
    same_user = user_ids[:, None] == user_ids[None, :]
    row_terms = jnp.sum(jnp.where(same_user, feat_gram * grad_gram, jnp.float32(0.0)), axis=1)
    user_sq = jnp.sum(jnp.where(same_user, row_terms[None, :], jnp.float32(0.0)), axis=1)
    user_count = clip_norms.shape[0]
    first_user = (row_index * lax.axis_size("col") + col_index) * user_count
    local_ids = user_ids - first_user
    one_hot = local_ids[:, None] == lax.broadcasted_iota(jnp.int32, (1, user_count), 1)
    user_bound = jnp.sum(jnp.where(one_hot, clip_norms[None, :], jnp.float32(0.0)), axis=1)
    factor = user_bound / jnp.maximum(jnp.sqrt(user_sq), user_bound)
    clipped = (factor[:, None] * embed_grad).astype(jnp.bfloat16)
    device_grad = lax.dot_general(
        image_feats, clipped, (((0,), (0,)), ((), ())), preferred_element_type=jnp.float32
    )
    grad_share = lax.psum_scatter(
        device_grad.reshape(-1, 128), ("row", "col"), scatter_dimension=0, tiled=True
    )
    new_grad_sum = grad_sum + grad_share
    update = new_grad_sum + tree_noise
    total_sq = lax.psum(jnp.sum(update * update), ("row", "col"))
    norm_cap = math.sqrt(projection.shape[0] * embed_width)
    shrink = norm_cap / jnp.maximum(jnp.sqrt(total_sq), norm_cap)
    theta_new = (init_weights - RATE * shrink * update).astype(jnp.bfloat16)
    gathered = lax.all_gather(theta_new, ("row", "col"), axis=0, tiled=True)
    new_weights = gathered.reshape(projection.shape[0], embed_width)
    return (new_weights, new_grad_sum)


def solution(mesh):
    in_specs = (
        P(("row", "col"), None),
        P(("row", "col"), None),
        P(),
        P(("row", "col")),
        P(("row", "col")),
        P(("row", "col"), None),
        P(("row", "col"), None),
        P(("row", "col"), None),
    )
    out_specs = (P(), P(("row", "col"), None))
    return jax.shard_map(body, mesh=mesh, in_specs=in_specs, out_specs=out_specs, check_vma=False)
```

profile of v0, /device:TPU:1, one launch (start us, length us, event | category | flops | bytes accessed | tf_op | source)
XLA Modules:
  0.0 1542.5 jit_solution(8835826427394815947)
XLA Ops:
  7.2 1.8 copy-done
  9.0 1.6 multiply_reduce_fusion.1
  10.6 0.8 multiply_convert_fusion.1
  11.5 1.1 fusion.13
  12.6 1.8 fusion.14
  14.5 41.3 %all-gather.5.cloned.1.call-done = bf16[2048,1024]{1,0:T(8,128)(2,1)} async-done(((bf16[128,1024]{1,0:T(8,128)(2,1)}), bf16[2048,1024]{1,0:T(8,128)(2,1)}) %all-gather.5.cloned.1.call-update) | async-done | bytes 4194320 | tf_op jit(solution)/shard_map/all_gather | solution.py:57
  55.8 77.3 %all-gather.7.cloned.1.call-done = bf16[2048,1024]{1,0:T(8,128)(2,1)} async-done(((bf16[128,1024]{1,0:T(8,128)(2,1)}), bf16[2048,1024]{1,0:T(8,128)(2,1)}) %all-gather.7.cloned.1.call-update) | async-done | bytes 4194320 | tf_op jit(solution)/shard_map/all_gather | solution.py:53
  133.1 25.7 %fusion.10 = f32[2048,1024]{1,0:T(8,128)} fusion(bf16[2048,1024]{1,0:T(8,128)(2,1)} %all-gather.7.cloned.1.call-done, bf16[2048,1024]{1,0:T(8,128)(2,1)} %all-gather.5.cloned.1.call-done, s32[2048]{0:T(1024)S(1)} %fusion.20, pred[2048]{0:T(1024)(128)(4,1)S(1)} %get-tuple-element.9, pred[2048]{0:T(1024)(128)(4,1)S(1)} %get-tuple-element.10), kind=kOutput, calls=%fused_computation.11 | convolution fusion | flops 17228103680 | bytes 16789504 | tf_op jit(solution)/shard_map/dot_general | solution.py:31
  158.9 0.6 copy-done.23
  159.6 1.4 fusion.24
  160.9 97.9 %reduce-scatter.4.cloned.1.call-done = f32[128,1024]{1,0:T(8,128)} async-done(((f32[2048,1024]{1,0:T(8,128)}), f32[128,1024]{1,0:T(8,128)}) %reduce-scatter.4.cloned.1.call-update) | async-done | bytes 524304 | tf_op jit(solution)/shard_map/reduce_scatter | solution.py:59
  258.8 1.2 multiply_reduce_fusion
  259.9 2.0 fusion.12
  262.0 0.1 fusion.16
  262.1 4.7 convolution_bitcast_fusion
  266.8 6.3 copy.12
  273.1 6.9 reshape.54
  280.0 657.9 %fusion = f32[48,128]{1,0:T(8,128)S(1)} fusion(f32[11264,128]{1,0:T(8,128)} %reshape.54), kind=kCustom, calls=%all-reduce-scatter | all-reduce-scatter fusion | flops 1572865 | bytes 5791744
  937.9 2.3 collective-permute-start
  940.2 1.9 collective-permute-start.21
  942.1 1.3 collective-permute-start.1
  943.4 1.5 collective-permute-start.10
  944.9 1.3 collective-permute-start.11
  946.2 1.3 collective-permute-start.12
  947.5 1.3 collective-permute-start.13
  948.8 1.3 collective-permute-start.14
  950.1 1.3 collective-permute-start.15
  951.5 1.3 collective-permute-start.16
  952.8 1.3 collective-permute-start.17
  954.1 1.3 collective-permute-start.18
  955.4 1.3 collective-permute-start.19
  956.7 13.2 collective-permute-start.2
  970.0 2.6 collective-permute-start.20
  972.7 1.3 collective-permute-start.3
  974.0 1.3 collective-permute-start.4
  975.3 4.2 collective-permute-start.5
  979.5 4.7 collective-permute-start.6
  984.2 1.4 collective-permute-start.7
  985.6 4.8 collective-permute-start.8
  990.4 30.0 %collective-permute-start.9 = (f32[48,128]{1,0:T(8,128)S(1)}, f32[48,128]{1,0:T(8,128)}, u32[]{:S(2)}, u32[]{:S(2)}) collective-permute-start(f32[48,128]{1,0:T(8,128)S(1)} %fusion), channel_id=1, source_target_pairs={{0,10},{1,11},{2,12},{3,13},{4,14},{5,15},{6,16},{7,17},{8,18},{9,... | collective-permute-start | bytes 73736
  1020.7 0.5 copy-done.19
  1021.3 0.6 copy-done.22
  1021.9 16.9 %concatenate = f32[1068,128]{1,0:T(8,128)S(1)} concatenate(f32[12,128]{1,0:T(8,128)} %collective-permute-done.21, f32[48,128]{1,0:T(8,128)} %copy-done.16, f32[48,128]{1,0:T(8,128)} %copy-done.14, f32[48,128]{1,0:T(8,128)} %copy-done.13, f32[48,128]{1,0:T(8,128)} %copy-done.12, f32[48,128]{1,0:T(8,128)} %copy-done.11, f32[48,128]{1,0:T(8,128)} %copy-done.10, ...), dimensions={0} | concatenate | bytes 1093632
  1038.8 1.2 multiply_reduce_fusion.2
  1040.0 80.5 %psum.7 = f32[]{:T(128)} all-reduce(f32[]{:T(128)} %get-tuple-element.2), channel_id=1, replica_groups=mesh['row'=16,'col'=16] {'row','col'}, use_global_device_ids=true, to_apply=%region_9.10 | all-reduce | flops 1 | bytes 8 | tf_op jit(solution)/shard_map/psum | solution.py:86
  1121.2 0.6 fusion.17
  1121.9 407.6 %all-gather.9.cloned.1.call-done = bf16[256,44,128]{2,1,0:T(8,128)(2,1)} async-done(((bf16[1,44,128]{2,1,0:T(8,128)(2,1)}), bf16[256,44,128]{2,1,0:T(8,128)(2,1)}) %all-gather.9.cloned.1.call-update) | async-done | bytes 2883600 | tf_op jit(solution)/shard_map/all_gather | solution.py:90
  1529.5 6.4 reshape.55
  (84 shorter events, 0.6 us)
Async XLA Ops:
  7.2 1.8 copy-start
  7.2 48.6 %all-gather.5.cloned.1.call-start = ((), (), s32[]{:S(2)}) async-start(), calls=%async_computation.1 | async-start | bytes 4456448 | tf_op jit(solution)/shard_map/all_gather | solution.py:57
  11.5 121.7 %all-gather.7.cloned.1.call-start = ((), (), s32[]{:S(2)}) async-start(), calls=%async_computation.2 | async-start | bytes 4456448 | tf_op jit(solution)/shard_map/all_gather | solution.py:53
  14.4 244.4 %reduce-scatter.4.cloned.1.call-start = ((), (), s32[]{:S(2)}) async-start(), calls=%async_computation.3 | async-start | bytes 8912896 | tf_op jit(solution)/shard_map/reduce_scatter | solution.py:59
  158.8 0.7 copy-start.23
  158.8 0.7 copy-start.24
  158.8 1370.7 %all-gather.9.cloned.1.call-start = ((), (), s32[]{:S(2)}) async-start(), calls=%async_computation.4 | async-start | bytes 3158016 | tf_op jit(solution)/shard_map/all_gather | solution.py:90
  280.0 758.7 %copy-start.2 = (f32[44,128]{1,0:T(8,128)S(1)}, f32[44,128]{1,0:T(8,128)}, u32[]{:S(2)}) copy-start(f32[44,128]{1,0:T(8,128)} %param.15) | copy-start | bytes 67588
  280.0 758.7 %copy-start.3 = (f32[44,128]{1,0:T(8,128)S(1)}, f32[44,128]{1,0:T(8,128)}, u32[]{:S(2)}) copy-start(f32[44,128]{1,0:T(8,128)} %param.13) | copy-start | bytes 67588
  280.0 841.2 %copy-start.1 = (f32[44,128]{1,0:T(8,128)S(1)}, f32[44,128]{1,0:T(8,128)}, u32[]{:S(2)}) copy-start(f32[44,128]{1,0:T(8,128)} %param.14) | copy-start | bytes 67588
  937.9 9.6 collective-permute-start
  940.2 5.9 collective-permute-start.21
  942.1 6.7 collective-permute-start.1
  943.4 6.7 collective-permute-start.10
  944.9 6.6 collective-permute-start.11
  946.2 6.6 collective-permute-start.12
  947.5 6.6 collective-permute-start.13
  948.8 41.6 %copy-start.4 = (f32[48,128]{1,0:T(8,128)}, f32[48,128]{1,0:T(8,128)S(1)}, u32[]{:S(2)}) copy-start(f32[48,128]{1,0:T(8,128)S(1)} %collective-permute-done.1) | copy-start | bytes 73732
  948.8 6.6 collective-permute-start.14
  950.1 70.3 %copy-start.5 = (f32[48,128]{1,0:T(8,128)}, f32[48,128]{1,0:T(8,128)S(1)}, u32[]{:S(2)}) copy-start(f32[48,128]{1,0:T(8,128)S(1)} %collective-permute-done.10) | copy-start | bytes 73732
  950.1 6.6 collective-permute-start.15
  951.5 69.0 %copy-start.6 = (f32[48,128]{1,0:T(8,128)}, f32[48,128]{1,0:T(8,128)S(1)}, u32[]{:S(2)}) copy-start(f32[48,128]{1,0:T(8,128)S(1)} %collective-permute-done.11) | copy-start | bytes 73732
  951.5 18.5 %collective-permute-start.16 = (f32[48,128]{1,0:T(8,128)S(1)}, f32[48,128]{1,0:T(8,128)S(1)}, u32[]{:S(2)}, u32[]{:S(2)}) collective-permute-start(f32[48,128]{1,0:T(8,128)S(1)} %fusion), channel_id=1, source_target_pairs={{0,17},{1,18},{2,19},{3,20},{4,21},{5,22},{6,23},{7,24},{8,25},{9,... | collective-permute-start | bytes 73736
  952.8 67.7 %copy-start.7 = (f32[48,128]{1,0:T(8,128)}, f32[48,128]{1,0:T(8,128)S(1)}, u32[]{:S(2)}) copy-start(f32[48,128]{1,0:T(8,128)S(1)} %collective-permute-done.12) | copy-start | bytes 73732
  952.8 19.9 %collective-permute-start.17 = (f32[48,128]{1,0:T(8,128)S(1)}, f32[48,128]{1,0:T(8,128)S(1)}, u32[]{:S(2)}, u32[]{:S(2)}) collective-permute-start(f32[48,128]{1,0:T(8,128)S(1)} %fusion), channel_id=1, source_target_pairs={{0,18},{1,19},{2,20},{3,21},{4,22},{5,23},{6,24},{7,25},{8,26},{9,... | collective-permute-start | bytes 73736
  954.1 66.4 %copy-start.8 = (f32[48,128]{1,0:T(8,128)}, f32[48,128]{1,0:T(8,128)S(1)}, u32[]{:S(2)}) copy-start(f32[48,128]{1,0:T(8,128)S(1)} %collective-permute-done.13) | copy-start | bytes 73732
  954.1 19.9 %collective-permute-start.18 = (f32[48,128]{1,0:T(8,128)S(1)}, f32[48,128]{1,0:T(8,128)S(1)}, u32[]{:S(2)}, u32[]{:S(2)}) collective-permute-start(f32[48,128]{1,0:T(8,128)S(1)} %fusion), channel_id=1, source_target_pairs={{0,19},{1,20},{2,21},{3,22},{4,23},{5,24},{6,25},{7,26},{8,27},{9,... | collective-permute-start | bytes 73736
  955.4 65.1 %copy-start.9 = (f32[48,128]{1,0:T(8,128)}, f32[48,128]{1,0:T(8,128)S(1)}, u32[]{:S(2)}) copy-start(f32[48,128]{1,0:T(8,128)S(1)} %collective-permute-done.14) | copy-start | bytes 73732
  955.4 19.9 %collective-permute-start.19 = (f32[48,128]{1,0:T(8,128)S(1)}, f32[48,128]{1,0:T(8,128)S(1)}, u32[]{:S(2)}, u32[]{:S(2)}) collective-permute-start(f32[48,128]{1,0:T(8,128)S(1)} %fusion), channel_id=1, source_target_pairs={{0,20},{1,21},{2,22},{3,23},{4,24},{5,25},{6,26},{7,27},{8,28},{9,... | collective-permute-start | bytes 73736
  956.7 63.8 %copy-start.10 = (f32[48,128]{1,0:T(8,128)}, f32[48,128]{1,0:T(8,128)S(1)}, u32[]{:S(2)}) copy-start(f32[48,128]{1,0:T(8,128)S(1)} %collective-permute-done.15) | copy-start | bytes 73732
  956.7 22.8 %collective-permute-start.2 = (f32[48,128]{1,0:T(8,128)S(1)}, f32[48,128]{1,0:T(8,128)S(1)}, u32[]{:S(2)}, u32[]{:S(2)}) collective-permute-start(f32[48,128]{1,0:T(8,128)S(1)} %fusion), channel_id=1, source_target_pairs={{0,3},{1,4},{2,5},{3,6},{4,7},{5,8},{6,9},{7,10},{8,11},{9,12},{10... | collective-permute-start | bytes 73736
  970.0 50.5 %copy-start.11 = (f32[48,128]{1,0:T(8,128)}, f32[48,128]{1,0:T(8,128)S(1)}, u32[]{:S(2)}) copy-start(f32[48,128]{1,0:T(8,128)S(1)} %collective-permute-done.16) | copy-start | bytes 73732
  970.0 14.2 collective-permute-start.20
  972.7 47.9 %copy-start.12 = (f32[48,128]{1,0:T(8,128)}, f32[48,128]{1,0:T(8,128)S(1)}, u32[]{:S(2)}) copy-start(f32[48,128]{1,0:T(8,128)S(1)} %collective-permute-done.17) | copy-start | bytes 73732
  972.7 13.0 collective-permute-start.3
  974.0 46.6 %copy-start.13 = (f32[48,128]{1,0:T(8,128)}, f32[48,128]{1,0:T(8,128)S(1)}, u32[]{:S(2)}) copy-start(f32[48,128]{1,0:T(8,128)S(1)} %collective-permute-done.18) | copy-start | bytes 73732
  974.0 16.4 %collective-permute-start.4 = (f32[48,128]{1,0:T(8,128)S(1)}, f32[48,128]{1,0:T(8,128)S(1)}, u32[]{:S(2)}, u32[]{:S(2)}) collective-permute-start(f32[48,128]{1,0:T(8,128)S(1)} %fusion), channel_id=1, source_target_pairs={{0,5},{1,6},{2,7},{3,8},{4,9},{5,10},{6,11},{7,12},{8,13},{9,14},{... | collective-permute-start | bytes 73736
  975.3 45.3 %copy-start.14 = (f32[48,128]{1,0:T(8,128)}, f32[48,128]{1,0:T(8,128)S(1)}, u32[]{:S(2)}) copy-start(f32[48,128]{1,0:T(8,128)S(1)} %collective-permute-done.19) | copy-start | bytes 73732
  975.3 45.3 %collective-permute-start.5 = (f32[48,128]{1,0:T(8,128)S(1)}, f32[48,128]{1,0:T(8,128)S(1)}, u32[]{:S(2)}, u32[]{:S(2)}) collective-permute-start(f32[48,128]{1,0:T(8,128)S(1)} %fusion), channel_id=1, source_target_pairs={{0,6},{1,7},{2,8},{3,9},{4,10},{5,11},{6,12},{7,13},{8,14},{9,15},... | collective-permute-start | bytes 73736
  979.5 41.0 %copy-start.15 = (f32[48,128]{1,0:T(8,128)}, f32[48,128]{1,0:T(8,128)S(1)}, u32[]{:S(2)}) copy-start(f32[48,128]{1,0:T(8,128)S(1)} %collective-permute-done.2) | copy-start | bytes 73732
  979.5 41.1 %collective-permute-start.6 = (f32[48,128]{1,0:T(8,128)S(1)}, f32[48,128]{1,0:T(8,128)S(1)}, u32[]{:S(2)}, u32[]{:S(2)}) collective-permute-start(f32[48,128]{1,0:T(8,128)S(1)} %fusion), channel_id=1, source_target_pairs={{0,7},{1,8},{2,9},{3,10},{4,11},{5,12},{6,13},{7,14},{8,15},{9,16}... | collective-permute-start | bytes 73736
  984.2 36.4 %copy-start.16 = (f32[48,128]{1,0:T(8,128)}, f32[48,128]{1,0:T(8,128)S(1)}, u32[]{:S(2)}) copy-start(f32[48,128]{1,0:T(8,128)S(1)} %collective-permute-done.20) | copy-start | bytes 73732
  984.2 36.4 %collective-permute-start.7 = (f32[48,128]{1,0:T(8,128)S(1)}, f32[48,128]{1,0:T(8,128)S(1)}, u32[]{:S(2)}, u32[]{:S(2)}) collective-permute-start(f32[48,128]{1,0:T(8,128)S(1)} %fusion), channel_id=1, source_target_pairs={{0,8},{1,9},{2,10},{3,11},{4,12},{5,13},{6,14},{7,15},{8,16},{9,17... | collective-permute-start | bytes 73736
  985.6 34.9 %copy-start.17 = (f32[48,128]{1,0:T(8,128)}, f32[48,128]{1,0:T(8,128)S(1)}, u32[]{:S(2)}) copy-start(f32[48,128]{1,0:T(8,128)S(1)} %collective-permute-done.3) | copy-start | bytes 73732
  985.6 35.0 %collective-permute-start.8 = (f32[48,128]{1,0:T(8,128)S(1)}, f32[48,128]{1,0:T(8,128)S(1)}, u32[]{:S(2)}, u32[]{:S(2)}) collective-permute-start(f32[48,128]{1,0:T(8,128)S(1)} %fusion), channel_id=1, source_target_pairs={{0,9},{1,10},{2,11},{3,12},{4,13},{5,14},{6,15},{7,16},{8,17},{9,1... | collective-permute-start | bytes 73736
  990.4 30.2 %copy-start.18 = (f32[48,128]{1,0:T(8,128)}, f32[48,128]{1,0:T(8,128)S(1)}, u32[]{:S(2)}) copy-start(f32[48,128]{1,0:T(8,128)S(1)} %collective-permute-done.4) | copy-start | bytes 73732
  990.4 31.4 %collective-permute-start.9 = (f32[48,128]{1,0:T(8,128)S(1)}, f32[48,128]{1,0:T(8,128)}, u32[]{:S(2)}, u32[]{:S(2)}) collective-permute-start(f32[48,128]{1,0:T(8,128)S(1)} %fusion), channel_id=1, source_target_pairs={{0,10},{1,11},{2,12},{3,13},{4,14},{5,15},{6,16},{7,17},{8,18},{9,... | collective-permute-start | bytes 73736
  1020.6 0.6 copy-start.19
  (3 other events, 1.8 us)
Sparse Core Ops, SparseCore 0:
  11.6 44.1 all-gather.4
  58.8 74.2 all-gather.6
  158.9 99.7 reduce-scatter.3
  1122.0 407.4 all-gather.8
where the time goes:
time: 1550 us; the launch traced here: 1540 us
  blocking collectives  738 us (48%)
  waiting for transfers between devices  624 us (40%)
  starting transfers between devices  82.2 us (5%)
  local copies, waits for them, and re-layouts  40.2 us (3%)
  matrix products  35.4 us (2%)
    unnamed x1, blocking collectives  658 us
    all_gather x1, waiting for transfers between devices, body(): gathered = lax.all_gather(theta_new, ('row', 'col'), axis=0, tiled=True)  408 us
    reduce_scatter x1, waiting for transfers between devices, body(): lax.psum_scatter(partial_value, 'col', scatter_dimension=0, tiled=True)  97.9 us
    unnamed x22, starting transfers between devices  82 us
    psum x1, blocking collectives, body(): total_sq = lax.psum(jnp.sum(update * update), ('row', 'col'))  80.5 us
    all_gather x1, waiting for transfers between devices, body(): text_block = lax.all_gather(text_unit, 'row', axis=0, tiled=True)  77.3 us
    all_gather x1, waiting for transfers between devices, body(): lax.all_gather(image_unit, 'col', axis=0, tiled=True)  41.3 us
  transfers between devices with their start and end apart: 26, of which 4 were waited for; matrix products, arithmetic and copies ran while one was open for 0% of the time, Pallas kernels for 0%

commit v1 on v0

v1 whole, which is shorter than its diff:
```python
import math

import jax
import jax.numpy as jnp
from jax import lax
from jax.experimental import pallas as pl
from jax.experimental.pallas import tpu as pltpu
from jax.sharding import PartitionSpec as P

LOGIT_SCALE = 32.0
LOGIT_BIAS = -5.0
RATE = 0.5
EPSILON = 1e-06

MESH = pl.DeviceIdType.MESH
X, Y, Z = 4, 4, 8
W, E, PAIRS, USERS = 1408, 1024, 128, 16
SHARE = W // X
BLOCK = SHARE // Z
PADDED = 48
WIDE = Z * PADDED
TEXTS = 2 * X * Y * PAIRS
CHUNK = 512
IMAGES = 2 * PAIRS
SLOT = E + 128
COPIES = 224
F32, BF16 = jnp.float32, jnp.bfloat16


def place():
    row, col = lax.axis_index("row"), lax.axis_index("col")
    x, zh = lax.div(row, 4), lax.rem(row, 4)
    y, zl, c = lax.div(col, 4), lax.rem(lax.div(col, 2), 2), lax.rem(col, 2)
    return x, y, zh * 2 + zl, c


def device(x, y, z, c):
    return (x * 4 + lax.div(z, 2), y * 4 + lax.rem(z, 2) * 2 + c)


def shift(value, by, size):
    return lax.rem(value + by, size)


class Copies:
    def __init__(self, send_sems, recv_sems):
        self.send_sems, self.recv_sems, self.used, self.all = send_sems, recv_sems, 0, []

    def reserve(self, count):
        self.used += count
        return self.used - count

    def make(self, src, dst, target, send_at, recv_at):
        return pltpu.make_async_remote_copy(
            src_ref=src,
            dst_ref=dst,
            send_sem=self.send_sems.at[send_at],
            recv_sem=self.recv_sems.at[recv_at],
            device_id=target,
            device_id_type=MESH,
        )

    def plan(self, src, dst, target):
        at = self.reserve(1)
        copy = self.make(src, dst, target, at, at)
        self.all.append(copy)
        return copy

    def push(self, src, dst, target):
        copy = self.plan(src, dst, target)
        copy.start()
        return copy

    def finish(self):
        for copy in self.all:
            copy.wait_send()


class Scatter:
    def __init__(self, net, src, dst, targets, is_self, mine):
        self.net, self.src, self.dst, self.targets, self.is_self, self.mine = net, src, dst, targets, is_self, mine
        self.at = net.reserve(8)

    def remote(self, i):
        return self.net.make(
            self.src.at[i], self.dst.at[self.mine], self.targets[i], self.at + i, self.at + self.mine
        )

    def local(self, i):
        sem = self.net.recv_sems.at[self.at + self.mine]
        return pltpu.make_async_copy(self.src.at[i], self.dst.at[self.mine], sem)

    def start(self):
        for i in range(8):
            pl.when(jnp.logical_not(self.is_self[i]))(self.remote(i).start)
            pl.when(self.is_self[i])(self.local(i).start)

    def wait(self):
        for i in range(8):
            self.net.make(self.src.at[i], self.dst.at[i], self.targets[i], self.at + i, self.at + i).wait_recv()

    def wait_sent(self):
        for i in range(8):
            pl.when(jnp.logical_not(self.is_self[i]))(self.remote(i).wait_send)


def kernel(
    feats_ref, text_ref, proj_hbm, norms_ref, ids_column, ids_row, state_ref,
    weights_ref, sums_ref,
    proj, texts, images, raw_ref, acc, own_grad, weigh0, weigh1,
    send_up, send_down, recv_up, recv_down,
    feats_all, clipped, clipped_all, spread, x_send, x_recv, z_part, z_recv, z_tiles,
    state_recv, state_tile, sums_send, sq_send, sq_recv,
    proj_sem, send_sems, recv_sems,
):
    x, y, z, c = place()
    col = lax.axis_index("col")
    k = c * 4 + y
    other = 1 - c
    zl = lax.rem(z, 2)
    at_x = [device(shift(x, o, X), y, z, c) for o in range(1, X)]
    at_y = [device(x, shift(y, o, Y), z, c) for o in range(1, Y)]
    at_z = [device(x, y, shift(z, o, Z), c) for o in range(1, Z)]
    across = device(x, y, z, other)
    at_y_across = [device(x, shift(y, o, Y), z, other) for o in range(1, Y)]
    flip = z + 1 - 2 * zl
    at_flip = [device(x, shift(y, o, Y), flip, cc) for o in range(Y) for cc in (c, other)][1:]
    x_up, x_down, y_up, y_down, z_up, z_down = at_x[0], at_x[2], at_y[0], at_y[2], at_z[0], at_z[6]

    load = pltpu.make_async_copy(proj_hbm, proj, proj_sem)
    load.start()
    text = text_ref[...].astype(F32)
    texts[0:PAIRS, :] = (
        text * lax.rsqrt(jnp.sum(text * text, axis=1, keepdims=True) + EPSILON)
    ).astype(BF16)

    barrier = pltpu.get_barrier_semaphore()
    partners = at_x + at_y + at_z + [across] + at_y_across + at_flip
    for target in partners:
        pl.semaphore_signal(barrier, inc=1, device_id=target, device_id_type=MESH)
    pl.semaphore_wait(barrier, len(partners))
    net = Copies(send_sems, recv_sems)

    def lanes(index, width=128):
        return pl.ds(pl.multiple_of(index * width, width), width)

    def slot(rx, ry, rows, core=0):
        base = (core * 16 + rx * 4 + ry) * PAIRS
        return texts.at[base + rows[0]:base + rows[1], :]

    def hop(axis, up, rx, ry, rows):
        step = 3 if up else 1
        if axis == "x":
            return net.plan(slot(rx, ry, rows), slot((rx + step) % 4, ry, rows), x_up if up else x_down)
        return net.plan(slot(rx, ry, rows), slot(rx, (ry + step) % 4, rows), y_up if up else y_down)

    crossings = []

    def cross(rx, ry, rows):
        crossings.append(net.push(slot(rx, ry, rows), slot(rx, ry, rows, 1), across))

    class Half:
        def __init__(self, first, second, low):
            self.rows, self.swap = (low, low + 64), first == "y"
            self.parts = ((low, low + 32), (low + 32, low + 64))
            r, p = self.rows, self.parts
            self.first = [hop(first, up, 0, 0, r) for up in (True, False)]
            self.relay = [hop(first, up, *self.at(3 if up else 1, 0), p[0 if up else 1]) for up in (True, False)]
            self.second = [[hop(second, up, *self.at(a, 0), r) for up in (True, False)] for a in range(4)]
            self.last = [
                [hop(second, up, *self.at(a, 3 if up else 1), p[0 if up else 1]) for up in (True, False)]
                for a in range(4)
            ]

        def at(self, a, b):
            return (b, a) if self.swap else (a, b)

        def open(self, a):
            for copy in self.second[a]:
                copy.start()

        def got_first(self, i):
            a = (3, 1)[i]
            self.first[i].wait_recv()
            self.relay[i].start()
            self.open(a)
            cross(*self.at(a, 0), self.rows)

        def got_relay(self):
            for copy in self.relay:
                copy.wait_recv()
            self.open(2)
            cross(*self.at(2, 0), self.rows)

        def got_second(self, a):
            for i in range(2):
                self.second[a][i].wait_recv()
                self.last[a][i].start()
                cross(*self.at(a, (3, 1)[i]), self.rows)

        def got_last(self, a):
            for copy in self.last[a]:
                copy.wait_recv()
            cross(*self.at(a, 2), self.rows)

    low, high = Half("x", "y", 0), Half("y", "x", 64)
    halves = (low, high)
    for half in halves:
        for copy in half.first:
            copy.start()
    for half in halves:
        half.open(0)
    cross(0, 0, (0, PAIRS))

    load.wait()
    raw = jnp.dot(feats_ref[...], proj[...], preferred_element_type=F32)
    raw_ref[...] = raw
    inverse = lax.rsqrt(jnp.sum(raw * raw, axis=1, keepdims=True) + EPSILON)

    def image(index, rows=(0, PAIRS)):
        return images.at[index * PAIRS + rows[0]:index * PAIRS + rows[1], :]

    images[PAIRS:2 * PAIRS, :] = (raw * inverse).astype(BF16)
    up = [net.plan(image(a), image(b), z_up) for a, b in ((1, 7), (7, 5), (5, 3))]
    down = [net.plan(image(a), image(b), z_down) for a, b in ((1, 6), (6, 4), (4, 2))]
    up.append(net.plan(image(3, (0, 64)), image(0, (0, 64)), z_up))
    down.append(net.plan(image(2, (64, 128)), image(0, (64, 128)), z_down))
    up[0].start()
    down[0].start()

    def turn(step):
        for ring in (up, down):
            ring[step].wait_recv()
            if step < 3:
                ring[step + 1].start()

    owner_slot = (lax.rem(y, 2) * 2 + zl) * 2 + c
    zh2 = z - zl
    half_y = lax.div(y, 2)
    state_out = Scatter(
        net, state_ref, state_recv,
        [device(x, i % 4, zh2 + half_y, i // 4) for i in range(8)],
        [jnp.logical_and(zl == half_y, k == i) for i in range(8)],
        owner_slot,
    )

    for half in halves:
        half.got_first(0)
        half.got_first(1)
    for half in halves:
        half.got_second(0)
    turn(0)
    for half in halves:
        half.got_relay()
    for half in halves:
        half.got_last(0)
    for a in (3, 1):
        for half in halves:
            half.got_second(a)
    turn(1)
    for half in halves:
        half.got_second(2)
    for a in (3, 1):
        for half in halves:
            half.got_last(a)
    turn(2)
    for half in halves:
        half.got_last(2)
    turn(3)
    for copy in crossings:
        copy.wait_recv()

    def feats_slot(ry, rows=(0, W)):
        return feats_all.at[rows[0]:rows[1], ry * PAIRS:(ry + 1) * PAIRS]

    feats_all[:, 0:PAIRS] = feats_ref[...].T
    feats_near = [net.plan(feats_slot(0), feats_slot(3), y_up), net.plan(feats_slot(0), feats_slot(1), y_down)]
    feats_far = [
        net.plan(feats_slot(3, (0, W // 2)), feats_slot(2, (0, W // 2)), y_up),
        net.plan(feats_slot(1, (W // 2, W)), feats_slot(2, (W // 2, W)), y_down),
    ]
    feats_cross = net.plan(feats_all.at[:, 0:512], feats_all.at[:, 512:1024], across)
    for copy in feats_near:
        copy.start()
    state_out.start()

    grads_up = [net.plan(send_up.at[0, 0:64], recv_up.at[0, 0:64], z_up)]
    grads_down = [net.plan(send_down.at[0, 0:64], recv_down.at[0, 0:64], z_down)]
    for i in range(1, 4):
        grads_up.append(net.plan(send_up.at[i], recv_up.at[i], z_up))
        grads_down.append(net.plan(send_down.at[i], recv_down.at[i], z_down))

    def pack(dst, full, unit):
        along = jnp.sum(full * unit, axis=1, keepdims=True).astype(BF16).astype(F32)
        dst[:, 0:E] = (full - along * unit).astype(BF16)
        dst[:, E:SLOT] = jnp.broadcast_to(along, (full.shape[0], 128)).astype(BF16)

    def unpack(src, unit):
        return src[:, 0:E].astype(F32) + src[:, E:SLOT].astype(F32)[:, 0:1] * unit

    def grid_step(step, carry):
        rows = pl.ds(pl.multiple_of(step * IMAGES, IMAGES), IMAGES)

        def chunk(n):
            return texts[pl.ds(pl.multiple_of(n * CHUNK, CHUNK), CHUNK), :]

        def weigh(n):
            cosine = lax.dot_general(
                images[rows, :], chunk(n), (((1,), (1,)), ((), ())), preferred_element_type=F32
            )
            return (0.5 + 0.5 * jnp.tanh(0.5 * LOGIT_SCALE * cosine + 0.5 * LOGIT_BIAS)).astype(BF16)

        def fold(weights, n):
            acc[...] += jnp.dot(weights[...], chunk(n), preferred_element_type=F32)

        weigh0[...] = weigh(0)
        acc[...] = jnp.zeros_like(acc)

        def two(h, carry):
            weigh1[...] = weigh(2 * h + 1)
            fold(weigh0, 2 * h)
            weigh0[...] = weigh(2 * h + 2)
            fold(weigh1, 2 * h + 1)
            return carry

        last = TEXTS // CHUNK - 1
        lax.fori_loop(0, last // 2, two, 0)
        weigh1[...] = weigh(last)
        fold(weigh0, last - 1)
        fold(weigh1, last)

        @pl.when(step == 0)
        def _():
            far = LOGIT_SCALE * acc[0:PAIRS, :]
            unit = images[0:PAIRS, :].astype(F32)
            pack(send_up.at[0, 0:64], far[0:64], unit[0:64])
            pack(send_down.at[0, 0:64], far[64:128], unit[64:128])
            grads_up[0].start()
            grads_down[0].start()
            unit = images[PAIRS:2 * PAIRS, :].astype(F32)
            text = texts[0:PAIRS, :].astype(F32)
            cosine = jnp.sum(unit * text, axis=1, keepdims=True)
            sigmoid = 0.5 + 0.5 * jnp.tanh(0.5 * LOGIT_SCALE * cosine + 0.5 * LOGIT_BIAS)
            change = (sigmoid - 1.0).astype(BF16).astype(F32) - sigmoid.astype(BF16).astype(F32)
            own_grad[...] = LOGIT_SCALE * (acc[PAIRS:2 * PAIRS, :] + change * text)
            for near, far_copy in zip(feats_near, feats_far):
                near.wait_recv()
                far_copy.start()

        for at in range(1, 4):

            @pl.when(step == at)
            def _(at=at):
                for side, sends, recvs, grads in (
                    (0, send_up, recv_up, grads_up), (1, send_down, recv_down, grads_down)
                ):
                    grads[at - 1].wait_recv()
                    first = (2 * at + side) * PAIRS
                    full = LOGIT_SCALE * acc[side * PAIRS:(side + 1) * PAIRS, :]
                    unit = images[first:first + PAIRS, :].astype(F32)
                    if at > 1:
                        pack(sends.at[at], full + unpack(recvs.at[at - 1], unit), unit)
                    else:
                        come = slice(64 * side, 64 * side + 64)
                        kept = slice(64 - 64 * side, 128 - 64 * side)
                        both = full[come] + unpack(recvs.at[0, 0:64], unit[come])
                        pack(sends.at[at, come], both, unit[come])
                        pack(sends.at[at, kept], full[kept], unit[kept])
                    grads[at].start()
                if at == 1:
                    for copy in feats_far:
                        copy.wait_recv()
                    feats_cross.start()

        return carry

    lax.fori_loop(0, 4, grid_step, 0)

    state_out.wait()
    state_tile[...] = jnp.zeros_like(state_tile)
    for piece in range(8):
        first = 11 * (piece // 2) + 5 * (piece % 2)
        for a in range(3):
            state_tile[a, first:first + 6, :] += state_recv[piece, a, 0:6, :]

    raw = raw_ref[...]
    inverse = lax.rsqrt(jnp.sum(raw * raw, axis=1, keepdims=True) + EPSILON)
    feat_gram = lax.dot_general(
        feats_ref[...], feats_ref[...], (((1,), (1,)), ((), ())), preferred_element_type=F32
    )
    same_user = ids_column[...] == ids_row[...]
    first_user = (lax.axis_index("row") * 16 + col) * USERS
    one_hot = (ids_column[...] - first_user) == lax.broadcasted_iota(jnp.int32, (PAIRS, USERS), 1)
    bound = jnp.sum(jnp.where(one_hot, norms_ref[...], 0.0), axis=1, keepdims=True)
    unit = images[PAIRS:2 * PAIRS, :].astype(F32)
    grads_up[3].wait_recv()
    grads_down[3].wait_recv()
    unit_grad = own_grad[...] + unpack(recv_up.at[3], unit) + unpack(recv_down.at[3], unit)
    inner = jnp.sum(raw * unit_grad, axis=1, keepdims=True)
    embed_grad = inverse * unit_grad - inverse * inverse * inverse * raw * inner
    grad_gram = lax.dot_general(
        embed_grad, embed_grad, (((1,), (1,)), ((), ())),
        precision=lax.Precision.HIGHEST, preferred_element_type=F32,
    )
    terms = jnp.sum(jnp.where(same_user, feat_gram * grad_gram, 0.0), axis=0, keepdims=True)
    user_sq = jnp.sum(jnp.where(same_user, terms, 0.0), axis=1, keepdims=True)
    factor = bound / jnp.maximum(jnp.sqrt(user_sq), bound)
    clipped[...] = (factor * embed_grad).astype(BF16)

    def rows_of(core, ry):
        return clipped_all.at[(core * 4 + ry) * PAIRS:(core * 4 + ry + 1) * PAIRS, :]

    parts = []
    for o in range(1, Y):
        parts.append(net.push(clipped.at[:, lanes(c * 4 + shift(y, o, Y))], rows_of(0, 4 - o), at_y[o - 1]))
        parts.append(net.push(clipped.at[:, lanes(other * 4 + shift(y, o, Y))], rows_of(1, 4 - o), at_y_across[o - 1]))
    parts.append(net.push(clipped.at[:, lanes(other * 4 + y)], rows_of(1, 0), across))
    clipped_all[0:PAIRS, :] = clipped[:, lanes(k)]
    spread[...] = jnp.zeros_like(spread)
    feats_cross.wait_recv()
    for copy in parts:
        copy.wait_recv()

    def share(index):
        block = feats_all[pl.ds(pl.multiple_of(index * SHARE, 16), SHARE), :]
        part = jnp.dot(block, clipped_all[...], preferred_element_type=F32)
        for piece in range(Z):
            spread[piece * PADDED:piece * PADDED + BLOCK, :] = part[piece * BLOCK:(piece + 1) * BLOCK]
        return spread[...]

    moves = []
    for o in range(1, X):
        x_send[o - 1] = share(shift(x, o, X)).astype(BF16)
        moves.append(net.push(x_send.at[o - 1], x_recv.at[o - 1], at_x[o - 1]))
    total = share(x)
    for o in range(1, X):
        moves[o - 1].wait_recv()
        total = total + x_recv[o - 1].astype(F32)
    z_part[...] = total

    def rows(index):
        return pl.ds(pl.multiple_of(index * PADDED, 16), PADDED)

    moves = [
        net.push(z_part.at[rows(shift(z, o, Z)), :], z_recv.at[o - 1], at_z[o - 1])
        for o in range(1, Z)
    ]
    grad = z_part[rows(z), :]
    for o in range(1, Z):
        moves[o - 1].wait_recv()
        grad = grad + z_recv[o - 1]

    new_sum = state_tile[0] + grad
    update = new_sum + state_tile[1]
    for piece in range(8):
        first = 11 * (piece // 2) + 5 * (piece % 2)
        sums_send[piece] = new_sum[first:first + 8]

    square = jnp.sum((update * update).reshape(PADDED // 8, 8, 128), axis=0)
    at = 0
    for stage, targets in enumerate((at_z, at_x, at_y + [across] + at_y_across)):
        sq_send[stage] = square
        moves = [
            net.push(sq_send.at[stage], sq_recv.at[at + i], target)
            for i, target in enumerate(targets)
        ]
        for i, copy in enumerate(moves):
            copy.wait_recv()
            square = square + sq_recv[at + i]
        at += len(targets)
    norm = jnp.sqrt(jnp.sum(square, keepdims=True))
    cap = math.sqrt(W * E)
    shrink = cap / jnp.maximum(norm, cap)
    tile = (state_tile[2] - RATE * shrink * update).astype(BF16)

    z_tiles[rows(z), :] = tile
    moves = [net.push(z_tiles.at[rows(z), :], z_tiles.at[rows(z), :], target) for target in at_z]
    sums_out = Scatter(
        net, sums_send, sums_ref,
        [device(x, 2 * zl + i // 4, zh2 + (i // 2) % 2, i % 2) for i in range(8)],
        [
            jnp.logical_and(half_y == zl, owner_slot == i) for i in range(8)
        ],
        k,
    )
    sums_out.start()
    for copy in moves:
        copy.wait_recv()
    whole = z_tiles[...].astype(F32)
    whole = jnp.concatenate([whole[piece * PADDED:piece * PADDED + BLOCK] for piece in range(Z)], axis=0)
    share_rows = pl.ds(pl.multiple_of(x * SHARE, 16), SHARE)
    weights_ref[share_rows, lanes(k)] = whole.astype(BF16)

    half_rows = SHARE // 2

    def part_rows(index, upper):
        return pl.ds(pl.multiple_of(index * SHARE + upper * half_rows, 16), half_rows)

    first = weights_ref.at[part_rows(x, 0), lanes(k)]
    second = weights_ref.at[part_rows(x, 1), lanes(k)]
    moves_y = [net.push(first, first, target) for target in at_y]
    moves_x = [net.push(second, second, target) for target in at_x]
    for copy in moves_y:
        copy.wait_recv()
    first = weights_ref.at[part_rows(x, 0), lanes(c, 512)]
    moves = [net.push(first, first, target) for target in at_x + [across]]
    for copy in moves_x:
        copy.wait_recv()
    for o in range(X):
        second = weights_ref.at[part_rows(shift(x, o, X), 1), lanes(k)]
        moves += [net.push(second, second, target) for target in at_y + [across]]
    for copy in moves:
        copy.wait_recv()
    last = []
    for o in range(1, X):
        piece = weights_ref.at[part_rows(shift(x, o, X), 0), lanes(c, 512)]
        last.append(net.push(piece, piece, across))
    for o in range(1, Y):
        for a in range(X):
            piece = weights_ref.at[part_rows(shift(x, a, X), 1), lanes(c * 4 + shift(y, o, Y))]
            last.append(net.push(piece, piece, across))
    for copy in last:
        copy.wait_recv()
    sums_out.wait()
    state_out.wait_sent()
    sums_out.wait_sent()
    net.finish()


def body(
    image_feats, text_emb, projection, clip_norms, user_ids, grad_sum, init_weights, tree_noise
):
    c = lax.rem(lax.axis_index("col"), 2)
    state = jnp.pad(jnp.stack([grad_sum, tree_noise, init_weights]), ((0, 0), (4, 4), (0, 0)))
    state = lax.dynamic_slice(state, (0, 4 - 4 * c, 0), (3, 48, 128))
    state = state.reshape(3, 6, 8, 128).transpose(2, 0, 1, 3)
    state = jnp.pad(state, ((0, 0), (0, 0), (0, 2), (0, 0)))
    vmem = pl.BlockSpec(memory_space=pltpu.VMEM)
    weights, sums = pl.pallas_call(
        kernel,
        out_shape=(
            jax.ShapeDtypeStruct((W, E), BF16),
            jax.ShapeDtypeStruct((8, 8, 128), F32),
        ),
        in_specs=[vmem, vmem, pl.BlockSpec(memory_space=pl.ANY), vmem, vmem, vmem, vmem],
        out_specs=(vmem, vmem),
        scratch_shapes=[
            pltpu.VMEM((W, E), BF16),
            pltpu.VMEM((TEXTS, E), BF16),
            pltpu.VMEM((Z * PAIRS, E), BF16),
            pltpu.VMEM((PAIRS, E), F32),
            pltpu.VMEM((IMAGES, E), F32),
            pltpu.VMEM((PAIRS, E), F32),
            pltpu.VMEM((IMAGES, CHUNK), BF16),
            pltpu.VMEM((IMAGES, CHUNK), BF16),
            pltpu.VMEM((4, PAIRS, SLOT), BF16),
            pltpu.VMEM((4, PAIRS, SLOT), BF16),
            pltpu.VMEM((4, PAIRS, SLOT), BF16),
            pltpu.VMEM((4, PAIRS, SLOT), BF16),
            pltpu.VMEM((W, 8 * PAIRS), BF16),
            pltpu.VMEM((PAIRS, E), BF16),
            pltpu.VMEM((8 * PAIRS, 128), BF16),
            pltpu.VMEM((WIDE, 128), F32),
            pltpu.VMEM((X - 1, WIDE, 128), BF16),
            pltpu.VMEM((X - 1, WIDE, 128), BF16),
            pltpu.VMEM((WIDE, 128), F32),
            pltpu.VMEM((Z - 1, PADDED, 128), F32),
            pltpu.VMEM((WIDE, 128), BF16),
            pltpu.VMEM((8, 3, 8, 128), F32),
            pltpu.VMEM((3, PADDED, 128), F32),
            pltpu.VMEM((8, 8, 128), F32),
            pltpu.VMEM((3, 8, 128), F32),
            pltpu.VMEM((17, 8, 128), F32),
            pltpu.SemaphoreType.DMA,
            pltpu.SemaphoreType.DMA((COPIES,)),
            pltpu.SemaphoreType.DMA((COPIES,)),
        ],
        compiler_params=pltpu.CompilerParams(
            collective_id=1, has_side_effects=True, vmem_limit_bytes=48 * 1024 * 1024
        ),
    )(
        image_feats, text_emb, projection, clip_norms.reshape(1, USERS),
        user_ids.reshape(PAIRS, 1), user_ids.reshape(1, PAIRS), state,
    )
    sums = sums[:, :6].transpose(1, 0, 2).reshape(48, 128)
    return weights, lax.dynamic_slice(sums, (4 * c, 0), (44, 128))


def solution(mesh):
    in_specs = (
        P(("row", "col"), None),
        P(("row", "col"), None),
        P(),
        P(("row", "col")),
        P(("row", "col")),
        P(("row", "col"), None),
        P(("row", "col"), None),
        P(("row", "col"), None),
    )
    out_specs = (P(), P(("row", "col"), None))
    return jax.shard_map(body, mesh=mesh, in_specs=in_specs, out_specs=out_specs, check_vma=False)
```

time: 1550 us -> 146 us (0.09)
  blocking collectives: 738 us -> 0 us
  waiting for transfers between devices: 624 us -> 0 us
  Pallas kernels: 0 us -> 138 us
  starting transfers between devices: 82.2 us -> 0 us
  matrix products: 35.4 us -> 0 us
  local copies, waits for them, and re-layouts: 40.2 us -> 6.24 us
    unnamed x1 -> x0, blocking collectives: 658 us -> none
    all_gather x3 -> x0, waiting for transfers between devices: 526 us -> none  [the longest x1 408 us: body(): gathered = lax.all_gather(theta_new, ('row', 'col'), axis=0, tiled=True)]
    pallas_call x0 -> x1, Pallas kernels: none -> 138 us  [body(): pl.pallas_call(kernel, out_shape=(jax.ShapeDtypeStruct((W, E), BF16), jax...]
    reduce_scatter x1 -> x0, waiting for transfers between devices: 97.9 us -> none  [body(): lax.psum_scatter(partial_value, 'col', scatter_dimension=0, tiled=True)]
    unnamed x22 -> x0, starting transfers between devices: 82 us -> none
    psum x1 -> x0, blocking collectives: 80.5 us -> none  [body(): total_sq = lax.psum(jnp.sum(update * update), ('row', 'col'))]
    dot_general x5 -> x0, matrix products: 35.4 us -> none  [the longest x1 25.7 us: fold_rows(): jnp.dot(pair_weight, text_block, preferred_element_type=jnp.float32)]
    unnamed x52 -> x9, local copies, waits for them, and re-layouts: 20.5 us -> 4.82 us
  transfers between devices with their start and end apart: 26 -> 0, of which waited for: 4 -> 0; matrix products, arithmetic and copies ran while one was open for 0% -> 0% of each run, Pallas kernels for 0% -> 0%
where the time goes in v1:
time: 146 us
  Pallas kernels  138 us (95%)
  local copies, waits for them, and re-layouts  6.24 us (4%)
    pallas_call x1, Pallas kernels, body(): pl.pallas_call(kernel, out_shape=(jax.ShapeDtypeStruct((W, E), BF16), jax...  138 us
    unnamed x9, local copies, waits for them, and re-layouts  4.82 us

profile of v1, /device:TPU:1, one launch (start us, length us, event | category | flops | bytes accessed | tf_op | source)
XLA Modules:
  0.0 145.7 jit_solution(3499624243763903684)
XLA Ops:
  0.6 0.8 copy.12.ids_column
  1.4 0.8 fusion.3
  2.3 0.0 copy-start
  2.3 1.0 copy-done
  3.3 0.0 copy-start.1
  3.3 0.9 copy-done.1
  4.2 0.0 copy-start.2
  4.2 0.7 copy-done.2
  4.9 0.0 copy-start.3
  4.9 0.7 copy-done.3
  5.5 138.0 %shard_map.95 = (bf16[1408,1024]{1,0:T(8,128)(2,1)S(1)}, f32[8,8,128]{2,1,0:T(8,128)S(1)}) custom-call(bf16[128,1408]{1,0:T(8,128)(2,1)S(1)} %copy-done, bf16[128,1024]{1,0:T(8,128)(2,1)S(1)} %copy-done.1, bf16[1408,1024]{1,0:T(8,128)(2,1)} %proj_hbm.1, f32[1,16]{1,0:T(1,128)S(1)} %bitcast.18, s32[128,1]{1,0:T(8,128)S(1)} %copy.12.ids_column, ...), custom_call_target="tpu_custom_call" | custom-call | tf_op jit(solution)/shard_map/pallas_call | solution.py:539
  143.5 0.6 constant_dynamic-slice_fusion
  144.2 1.6 %copy.19 = bf16[1408,1024]{1,0:T(8,128)(2,1)} copy(bf16[1408,1024]{1,0:T(8,128)(2,1)S(1)} %get-tuple-element.8) | data formatting | bytes 5767168
  (4 shorter events, 0.0 us)
Async XLA Ops:
  2.3 1.0 copy-start
  3.3 0.9 copy-start.1
  4.2 0.7 copy-start.2
  4.9 0.7 copy-start.3

commit v2 on v1

--- a/solution.py
+++ b/solution.py
@@ -20,10 +20,10 @@
 PADDED = 48
 WIDE = Z * PADDED
 TEXTS = 2 * X * Y * PAIRS
-CHUNK = 512
+CHUNK = 2048
 IMAGES = 2 * PAIRS
 SLOT = E + 128
-COPIES = 224
+COPIES = 240
 F32, BF16 = jnp.float32, jnp.bfloat16
 
 
@@ -105,13 +105,13 @@
 
 
 def kernel(
-    feats_ref, text_ref, proj_hbm, norms_ref, ids_column, ids_row, state_ref,
+    feats_hbm, text_hbm, proj_hbm, norms_hbm, ids_hbm, state_hbm,
     weights_ref, sums_ref,
-    proj, texts, images, raw_ref, acc, own_grad, weigh0, weigh1,
+    feats_ref, text_ref, norms_ref, ids_row, state_ref, proj, texts, images, raw_ref, acc, own_grad, weigh0, weigh1,
     send_up, send_down, recv_up, recv_down,
     feats_all, clipped, clipped_all, spread, x_send, x_recv, z_part, z_recv, z_tiles,
     state_recv, state_tile, sums_send, sq_send, sq_recv,
-    proj_sem, send_sems, recv_sems,
+    load_sems, send_sems, recv_sems,
 ):
     x, y, z, c = place()
     col = lax.axis_index("col")
@@ -127,8 +127,16 @@
     at_flip = [device(x, shift(y, o, Y), flip, cc) for o in range(Y) for cc in (c, other)][1:]
     x_up, x_down, y_up, y_down, z_up, z_down = at_x[0], at_x[2], at_y[0], at_y[2], at_z[0], at_z[6]
 
-    load = pltpu.make_async_copy(proj_hbm, proj, proj_sem)
-    load.start()
+    loads = [
+        pltpu.make_async_copy(src, dst, load_sems.at[i])
+        for i, (src, dst) in enumerate((
+            (text_hbm, text_ref), (feats_hbm, feats_ref), (proj_hbm, proj),
+            (state_hbm, state_ref), (norms_hbm, norms_ref), (ids_hbm, ids_row),
+        ))
+    ]
+    for load in loads:
+        load.start()
+    loads[0].wait()
     text = text_ref[...].astype(F32)
     texts[0:PAIRS, :] = (
         text * lax.rsqrt(jnp.sum(text * text, axis=1, keepdims=True) + EPSILON)
@@ -212,7 +220,8 @@
         half.open(0)
     cross(0, 0, (0, PAIRS))
 
-    load.wait()
+    for load in loads[1:]:
+        load.wait()
     raw = jnp.dot(feats_ref[...], proj[...], preferred_element_type=F32)
     raw_ref[...] = raw
     inverse = lax.rsqrt(jnp.sum(raw * raw, axis=1, keepdims=True) + EPSILON)
@@ -298,39 +307,38 @@
     def unpack(src, unit):
         return src[:, 0:E].astype(F32) + src[:, E:SLOT].astype(F32)[:, 0:1] * unit
 
-    def grid_step(step, carry):
-        rows = pl.ds(pl.multiple_of(step * IMAGES, IMAGES), IMAGES)
-
-        def chunk(n):
-            return texts[pl.ds(pl.multiple_of(n * CHUNK, CHUNK), CHUNK), :]
-
-        def weigh(n):
-            cosine = lax.dot_general(
-                images[rows, :], chunk(n), (((1,), (1,)), ((), ())), preferred_element_type=F32
-            )
-            return (0.5 + 0.5 * jnp.tanh(0.5 * LOGIT_SCALE * cosine + 0.5 * LOGIT_BIAS)).astype(BF16)
-
-        def fold(weights, n):
-            acc[...] += jnp.dot(weights[...], chunk(n), preferred_element_type=F32)
-
-        weigh0[...] = weigh(0)
+    def weigh(step, n):
+        rows = slice(step * IMAGES, (step + 1) * IMAGES)
+        cosine = lax.dot_general(
+            images[rows, :], texts[pl.ds(pl.multiple_of(n * CHUNK, CHUNK), CHUNK), :],
+            (((1,), (1,)), ((), ())), preferred_element_type=F32,
+        )
+        pair = 0.5 + 0.5 * jnp.tanh(0.5 * LOGIT_SCALE * cosine + 0.5 * LOGIT_BIAS)
+        (weigh0, weigh1)[step % 2][:, lanes(n, CHUNK)] = pair.astype(BF16)
+
+    def fold(step, n):
+        acc[...] += jnp.dot(
+            (weigh0, weigh1)[step % 2][:, lanes(n, CHUNK)],
+            texts[pl.ds(pl.multiple_of(n * CHUNK, CHUNK), CHUNK), :],
+            preferred_element_type=F32,
+        )
+
+    def first_weights(n, carry):
+        weigh(0, n)
+        return carry
+
+    lax.fori_loop(0, TEXTS // CHUNK, first_weights, 0)
+    for step in range(4):
         acc[...] = jnp.zeros_like(acc)
 
-        def two(h, carry):
-            weigh1[...] = weigh(2 * h + 1)
-            fold(weigh0, 2 * h)
-            weigh0[...] = weigh(2 * h + 2)
-            fold(weigh1, 2 * h + 1)
+        def part(n, carry, step=step):
+            if step < 3:
+                weigh(step + 1, n)
+            fold(step, n)
             return carry
 
-        last = TEXTS // CHUNK - 1
-        lax.fori_loop(0, last // 2, two, 0)
-        weigh1[...] = weigh(last)
-        fold(weigh0, last - 1)
-        fold(weigh1, last)
-
-        @pl.when(step == 0)
-        def _():
+        lax.fori_loop(0, TEXTS // CHUNK, part, 0)
+        if step == 0:
             far = LOGIT_SCALE * acc[0:PAIRS, :]
             unit = images[0:PAIRS, :].astype(F32)
             pack(send_up.at[0, 0:64], far[0:64], unit[0:64])
@@ -346,35 +354,27 @@
             for near, far_copy in zip(feats_near, feats_far):
                 near.wait_recv()
                 far_copy.start()
-
-        for at in range(1, 4):
-
-            @pl.when(step == at)
-            def _(at=at):
-                for side, sends, recvs, grads in (
-                    (0, send_up, recv_up, grads_up), (1, send_down, recv_down, grads_down)
-                ):
-                    grads[at - 1].wait_recv()
-                    first = (2 * at + side) * PAIRS
-                    full = LOGIT_SCALE * acc[side * PAIRS:(side + 1) * PAIRS, :]
-                    unit = images[first:first + PAIRS, :].astype(F32)
-                    if at > 1:
-                        pack(sends.at[at], full + unpack(recvs.at[at - 1], unit), unit)
-                    else:
-                        come = slice(64 * side, 64 * side + 64)
-                        kept = slice(64 - 64 * side, 128 - 64 * side)
-                        both = full[come] + unpack(recvs.at[0, 0:64], unit[come])
-                        pack(sends.at[at, come], both, unit[come])
-                        pack(sends.at[at, kept], full[kept], unit[kept])
-                    grads[at].start()
-                if at == 1:
-                    for copy in feats_far:
-                        copy.wait_recv()
-                    feats_cross.start()
-
-        return carry
-
-    lax.fori_loop(0, 4, grid_step, 0)
+            continue
+        for side, sends, recvs, grads in (
+            (0, send_up, recv_up, grads_up), (1, send_down, recv_down, grads_down)
+        ):
+            grads[step - 1].wait_recv()
+            first = (2 * step + side) * PAIRS
+            full = LOGIT_SCALE * acc[side * PAIRS:(side + 1) * PAIRS, :]
+            unit = images[first:first + PAIRS, :].astype(F32)
+            if step > 1:
+                pack(sends.at[step], full + unpack(recvs.at[step - 1], unit), unit)
+            else:
+                come = slice(64 * side, 64 * side + 64)
+                kept = slice(64 - 64 * side, 128 - 64 * side)
+                both = full[come] + unpack(recvs.at[0, 0:64], unit[come])
+                pack(sends.at[step, come], both, unit[come])
+                pack(sends.at[step, kept], full[kept], unit[kept])
+            grads[step].start()
+        if step == 1:
+            for copy in feats_far:
+                copy.wait_recv()
+            feats_cross.start()
 
     state_out.wait()
     state_tile[...] = jnp.zeros_like(state_tile)
@@ -388,10 +388,15 @@
     feat_gram = lax.dot_general(
         feats_ref[...], feats_ref[...], (((1,), (1,)), ((), ())), preferred_element_type=F32
     )
-    same_user = ids_column[...] == ids_row[...]
-    first_user = (lax.axis_index("row") * 16 + col) * USERS
-    one_hot = (ids_column[...] - first_user) == lax.broadcasted_iota(jnp.int32, (PAIRS, USERS), 1)
-    bound = jnp.sum(jnp.where(one_hot, norms_ref[...], 0.0), axis=1, keepdims=True)
+    local_row = (ids_row[...] - (lax.axis_index("row") * 16 + col) * USERS).astype(F32)
+    square_shape = (PAIRS, PAIRS)
+    diagonal = lax.broadcasted_iota(jnp.int32, square_shape, 0) == lax.broadcasted_iota(
+        jnp.int32, square_shape, 1
+    )
+    local_column = jnp.sum(jnp.where(diagonal, local_row, 0.0), axis=1, keepdims=True)
+    same_user = local_column == local_row
+    users = lax.broadcasted_iota(jnp.int32, (PAIRS, USERS), 1).astype(F32)
+    bound = jnp.sum(jnp.where(local_column == users, norms_ref[...], 0.0), axis=1, keepdims=True)
     unit = images[PAIRS:2 * PAIRS, :].astype(F32)
     grads_up[3].wait_recv()
     grads_down[3].wait_recv()
@@ -502,24 +507,51 @@
     moves_x = [net.push(second, second, target) for target in at_x]
     for copy in moves_y:
         copy.wait_recv()
-    first = weights_ref.at[part_rows(x, 0), lanes(c, 512)]
-    moves = [net.push(first, first, target) for target in at_x + [across]]
+    crossings = []
+
+    def give(piece):
+        crossings.append(net.push(piece, piece, across))
+
+    def low_piece(index, rows=(0, half_rows)):
+        start = pl.multiple_of(index * SHARE + rows[0], 16)
+        return weights_ref.at[pl.ds(start, rows[1] - rows[0]), lanes(c, 512)]
+
+    def high_piece(index, away):
+        return weights_ref.at[part_rows(shift(x, index, X), 1), lanes(c * 4 + shift(y, away, Y))]
+
+    low_moves = [net.push(low_piece(x), low_piece(x), target) for target in (x_up, x_down)]
+    give(low_piece(x))
     for copy in moves_x:
         copy.wait_recv()
-    for o in range(X):
-        second = weights_ref.at[part_rows(shift(x, o, X), 1), lanes(k)]
-        moves += [net.push(second, second, target) for target in at_y + [across]]
-    for copy in moves:
-        copy.wait_recv()
-    last = []
-    for o in range(1, X):
-        piece = weights_ref.at[part_rows(shift(x, o, X), 0), lanes(c, 512)]
-        last.append(net.push(piece, piece, across))
-    for o in range(1, Y):
+    high_moves = [
+        [net.push(high_piece(a, 0), high_piece(a, 0), target) for a in range(X)]
+        for target in (y_up, y_down)
+    ]
+    for a in range(X):
+        give(high_piece(a, 0))
+    low_relays, high_relays = [], []
+    for copy, away, rows_sent, target in (
+        (low_moves[0], 3, (0, 96), x_up), (low_moves[1], 1, (96, half_rows), x_down)
+    ):
+        copy.wait_recv()
+        index = shift(x, away, X)
+        low_relays.append(net.push(low_piece(index, rows_sent), low_piece(index, rows_sent), target))
+        give(low_piece(index))
+    for copies, away, sent, target in ((high_moves[0], 3, (0, 1), y_up), (high_moves[1], 1, (2, 3), y_down)):
+        for copy in copies:
+            copy.wait_recv()
+        for a in sent:
+            high_relays.append(net.push(high_piece(a, away), high_piece(a, away), target))
         for a in range(X):
-            piece = weights_ref.at[part_rows(shift(x, a, X), 1), lanes(c * 4 + shift(y, o, Y))]
-            last.append(net.push(piece, piece, across))
-    for copy in last:
+            give(high_piece(a, away))
+    for copy in low_relays:
+        copy.wait_recv()
+    give(low_piece(shift(x, 2, X)))
+    for copy in high_relays:
+        copy.wait_recv()
+    for a in range(X):
+        give(high_piece(a, 2))
+    for copy in crossings:
         copy.wait_recv()
     sums_out.wait()
     state_out.wait_sent()
@@ -542,17 +574,22 @@
             jax.ShapeDtypeStruct((W, E), BF16),
             jax.ShapeDtypeStruct((8, 8, 128), F32),
         ),
-        in_specs=[vmem, vmem, pl.BlockSpec(memory_space=pl.ANY), vmem, vmem, vmem, vmem],
+        in_specs=[pl.BlockSpec(memory_space=pl.ANY)] * 6,
         out_specs=(vmem, vmem),
         scratch_shapes=[
+            pltpu.VMEM((PAIRS, W), BF16),
+            pltpu.VMEM((PAIRS, E), BF16),
+            pltpu.VMEM((1, USERS), F32),
+            pltpu.VMEM((1, PAIRS), jnp.int32),
+            pltpu.VMEM((8, 3, 8, 128), F32),
             pltpu.VMEM((W, E), BF16),
             pltpu.VMEM((TEXTS, E), BF16),
             pltpu.VMEM((Z * PAIRS, E), BF16),
             pltpu.VMEM((PAIRS, E), F32),
             pltpu.VMEM((IMAGES, E), F32),
             pltpu.VMEM((PAIRS, E), F32),
-            pltpu.VMEM((IMAGES, CHUNK), BF16),
-            pltpu.VMEM((IMAGES, CHUNK), BF16),
+            pltpu.VMEM((IMAGES, TEXTS), BF16),
+            pltpu.VMEM((IMAGES, TEXTS), BF16),
             pltpu.VMEM((4, PAIRS, SLOT), BF16),
             pltpu.VMEM((4, PAIRS, SLOT), BF16),
             pltpu.VMEM((4, PAIRS, SLOT), BF16),
@@ -571,7 +608,7 @@
             pltpu.VMEM((8, 8, 128), F32),
             pltpu.VMEM((3, 8, 128), F32),
             pltpu.VMEM((17, 8, 128), F32),
-            pltpu.SemaphoreType.DMA,
+            pltpu.SemaphoreType.DMA((6,)),
             pltpu.SemaphoreType.DMA((COPIES,)),
             pltpu.SemaphoreType.DMA((COPIES,)),
         ],
@@ -580,7 +617,7 @@
         ),
     )(
         image_feats, text_emb, projection, clip_norms.reshape(1, USERS),
-        user_ids.reshape(PAIRS, 1), user_ids.reshape(1, PAIRS), state,
+        user_ids.reshape(1, PAIRS), state,
     )
     sums = sums[:, :6].transpose(1, 0, 2).reshape(48, 128)
     return weights, lax.dynamic_slice(sums, (4 * c, 0), (44, 128))

time: 146 us -> 142 us (0.973)
  Pallas kernels: 138 us -> 134 us
    pallas_call x1, Pallas kernels: 138 us -> 134 us  [body(): pl.pallas_call(kernel, out_shape=(jax.ShapeDtypeStruct((W, E), BF16), jax...]
where the time goes in v2:
time: 142 us; the launch traced here: 141 us
  Pallas kernels  134 us (94%)
  local copies, waits for them, and re-layouts  5.48 us (4%)
    pallas_call x1, Pallas kernels, body(): pl.pallas_call(kernel, out_shape=(jax.ShapeDtypeStruct((W, E), BF16), jax...  134 us
    unnamed x9, local copies, waits for them, and re-layouts  4.82 us

profile of v2, /device:TPU:1, one launch (start us, length us, event | category | flops | bytes accessed | tf_op | source)
XLA Modules:
  0.0 141.3 jit_solution(2901909746039856035)
XLA Ops:
  0.6 0.8 fusion.3
  1.5 0.0 copy-start
  1.5 1.0 copy-done
  2.5 0.0 copy-start.1
  2.5 0.9 copy-done.1
  3.4 0.0 copy-start.2
  3.4 0.7 copy-done.2
  4.1 0.0 copy-start.3
  4.1 0.7 copy-done.3
  4.8 134.3 %shard_map.95 = (bf16[1408,1024]{1,0:T(8,128)(2,1)S(1)}, f32[8,8,128]{2,1,0:T(8,128)S(1)}) custom-call(bf16[128,1408]{1,0:T(8,128)(2,1)S(1)} %copy-done, bf16[128,1024]{1,0:T(8,128)(2,1)S(1)} %copy-done.1, bf16[1408,1024]{1,0:T(8,128)(2,1)} %proj_hbm.1, f32[1,16]{1,0:T(1,128)S(1)} %bitcast.15, s32[1,128]{1,0:T(1,128)S(1)} %bitcast.16, ...), custom_call_target="tpu_custom_call" | custom-call | tf_op jit(solution)/shard_map/pallas_call | solution.py:571
  139.1 0.6 constant_dynamic-slice_fusion
  139.7 1.6 %copy.17 = bf16[1408,1024]{1,0:T(8,128)(2,1)} copy(bf16[1408,1024]{1,0:T(8,128)(2,1)S(1)} %get-tuple-element.8) | data formatting | bytes 5767168
  (4 shorter events, 0.0 us)
Async XLA Ops:
  1.5 1.0 copy-start
  2.5 0.9 copy-start.1
  3.4 0.7 copy-start.2
  4.1 0.7 copy-start.3

commit v3 on v2

--- a/solution.py
+++ b/solution.py
@@ -11,6 +11,7 @@
 LOGIT_BIAS = -5.0
 RATE = 0.5
 EPSILON = 1e-06
+LOG2_E = math.log2(math.e)
 
 MESH = pl.DeviceIdType.MESH
 X, Y, Z = 4, 4, 8
@@ -20,8 +21,8 @@
 PADDED = 48
 WIDE = Z * PADDED
 TEXTS = 2 * X * Y * PAIRS
-CHUNK = 2048
-IMAGES = 2 * PAIRS
+CHUNK = 512
+IMAGES = 4 * PAIRS
 SLOT = E + 128
 COPIES = 240
 F32, BF16 = jnp.float32, jnp.bfloat16
@@ -32,6 +33,11 @@
     x, zh = lax.div(row, 4), lax.rem(row, 4)
     y, zl, c = lax.div(col, 4), lax.rem(lax.div(col, 2), 2), lax.rem(col, 2)
     return x, y, zh * 2 + zl, c
+
+
+def sigmoid_of(cosine):
+    power = cosine * (-LOGIT_SCALE * LOG2_E) + (-LOGIT_BIAS * LOG2_E)
+    return pl.reciprocal(1.0 + jnp.exp2(power), approx=True)
 
 
 def device(x, y, z, c):
@@ -162,10 +168,11 @@
             return net.plan(slot(rx, ry, rows), slot((rx + step) % 4, ry, rows), x_up if up else x_down)
         return net.plan(slot(rx, ry, rows), slot(rx, (ry + step) % 4, rows), y_up if up else y_down)
 
-    crossings = []
+    crossings = [[] for _ in range(X)]
 
     def cross(rx, ry, rows):
-        crossings.append(net.push(slot(rx, ry, rows), slot(rx, ry, rows, 1), across))
+        crossings[rx].append(net.plan(slot(rx, ry, rows), slot(rx, ry, rows, 1), across))
+        return crossings[rx][-1]
 
     class Half:
         def __init__(self, first, second, low):
@@ -179,6 +186,9 @@
                 [hop(second, up, *self.at(a, 3 if up else 1), p[0 if up else 1]) for up in (True, False)]
                 for a in range(4)
             ]
+            self.cross = [
+                [cross(*self.at(a, b), r) if a or b else None for b in range(4)] for a in range(4)
+            ]
 
         def at(self, a, b):
             return (b, a) if self.swap else (a, b)
@@ -192,24 +202,24 @@
             self.first[i].wait_recv()
             self.relay[i].start()
             self.open(a)
-            cross(*self.at(a, 0), self.rows)
+            self.cross[a][0].start()
 
         def got_relay(self):
             for copy in self.relay:
                 copy.wait_recv()
             self.open(2)
-            cross(*self.at(2, 0), self.rows)
+            self.cross[2][0].start()
 
         def got_second(self, a):
             for i in range(2):
                 self.second[a][i].wait_recv()
                 self.last[a][i].start()
-                cross(*self.at(a, (3, 1)[i]), self.rows)
+                self.cross[a][(3, 1)[i]].start()
 
         def got_last(self, a):
             for copy in self.last[a]:
                 copy.wait_recv()
-            cross(*self.at(a, 2), self.rows)
+            self.cross[a][2].start()
 
     low, high = Half("x", "y", 0), Half("y", "x", 64)
     halves = (low, high)
@@ -218,7 +228,7 @@
             copy.start()
     for half in halves:
         half.open(0)
-    cross(0, 0, (0, PAIRS))
+    cross(0, 0, (0, PAIRS)).start()
 
     for load in loads[1:]:
         load.wait()
@@ -269,15 +279,15 @@
     turn(1)
     for half in halves:
         half.got_second(2)
-    for a in (3, 1):
+    turn(2)
+
+    def got_last(a):
         for half in halves:
             half.got_last(a)
-    turn(2)
-    for half in halves:
-        half.got_last(2)
-    turn(3)
-    for copy in crossings:
-        copy.wait_recv()
+
+    def got_cross(rx):
+        for copy in crossings[rx]:
+            copy.wait_recv()
 
     def feats_slot(ry, rows=(0, W)):
         return feats_all.at[rows[0]:rows[1], ry * PAIRS:(ry + 1) * PAIRS]
@@ -289,15 +299,15 @@
         net.plan(feats_slot(1, (W // 2, W)), feats_slot(2, (W // 2, W)), y_down),
     ]
     feats_cross = net.plan(feats_all.at[:, 0:512], feats_all.at[:, 512:1024], across)
-    for copy in feats_near:
-        copy.start()
-    state_out.start()
-
-    grads_up = [net.plan(send_up.at[0, 0:64], recv_up.at[0, 0:64], z_up)]
-    grads_down = [net.plan(send_down.at[0, 0:64], recv_down.at[0, 0:64], z_down)]
-    for i in range(1, 4):
-        grads_up.append(net.plan(send_up.at[i], recv_up.at[i], z_up))
-        grads_down.append(net.plan(send_down.at[i], recv_down.at[i], z_down))
+    def feats_on():
+        for near, far in zip(feats_near, feats_far):
+            near.wait_recv()
+            far.start()
+
+    def feats_over():
+        for copy in feats_far:
+            copy.wait_recv()
+        feats_cross.start()
 
     def pack(dst, full, unit):
         along = jnp.sum(full * unit, axis=1, keepdims=True).astype(BF16).astype(F32)
@@ -307,74 +317,102 @@
     def unpack(src, unit):
         return src[:, 0:E].astype(F32) + src[:, E:SLOT].astype(F32)[:, 0:1] * unit
 
-    def weigh(step, n):
-        rows = slice(step * IMAGES, (step + 1) * IMAGES)
+    class Side:
+        def __init__(self, first, come, sends, recvs, target):
+            self.blocks, self.sends, self.recvs = (0, first, first + 2, first + 4), sends, recvs
+            self.rows = ((64 - come, 128 - come), (come, come + 64))
+            self.copies = [net.plan(sends.at[i], recvs.at[i], target) for i in range(7)]
+
+        def give(self, hop, late):
+            i = 2 * hop - 1 + late
+            base = self.blocks[hop] * PAIRS
+            start, stop = self.rows[late]
+            unit = images[base + start:base + stop, :].astype(F32)
+            full = LOGIT_SCALE * acc[base + start:base + stop, :]
+            if hop > 1 or (hop == 1 and late):
+                come = i - 2
+                self.copies[come].wait_recv()
+                full = full + unpack(self.recvs.at[come], unit)
+            pack(self.sends.at[i], full, unit)
+            self.copies[i].start()
+
+    sides = (Side(2, 0, send_up, recv_up, z_up), Side(3, 64, send_down, recv_down, z_down))
+
+    def give(hop, late):
+        for side in sides:
+            side.give(hop, late)
+
+    def open_sums():
+        give(0, 1)
+        give(1, 0)
+
+    schedule = {
+        1: [lambda: got_last(3), lambda: got_last(1)],
+        3: [lambda: got_last(2)],
+        4: [lambda: turn(3), lambda: [copy.start() for copy in feats_near], state_out.start],
+        8: [lambda: got_cross(0), feats_on],
+        9: [lambda: got_cross(3)],
+        10: [lambda: got_cross(1)],
+        11: [lambda: got_cross(2)],
+        13: [open_sums, feats_over],
+        15: [lambda: give(1, 1)],
+    }
+    acc[...] = jnp.zeros_like(acc)
+
+    def run_events(s, which):
+        for at in which:
+            if at in schedule:
+
+                @pl.when(s == at)
+                def _(events=schedule[at]):
+                    for event in events:
+                        event()
+
+    def where(s):
+        quarter, turn_at = lax.div(s, 4), lax.rem(s, 4)
+        near = jnp.logical_or(quarter == 0, quarter == 3)
+        rx = lax.select(turn_at == 0, 0, lax.select(turn_at == 1, 3, turn_at - 1))
+        rows = pl.ds(pl.multiple_of(lax.select(near, IMAGES, 0), IMAGES), IMAGES)
+        base = (lax.div(quarter, 2) * 4 + rx) * CHUNK
+        return rows, pl.ds(pl.multiple_of(base, CHUNK), CHUNK)
+
+    def weigh(s, dst):
+        rows, block = where(s)
         cosine = lax.dot_general(
-            images[rows, :], texts[pl.ds(pl.multiple_of(n * CHUNK, CHUNK), CHUNK), :],
-            (((1,), (1,)), ((), ())), preferred_element_type=F32,
+            images[rows, :], texts[block, :], (((1,), (1,)), ((), ())), preferred_element_type=F32
         )
-        pair = 0.5 + 0.5 * jnp.tanh(0.5 * LOGIT_SCALE * cosine + 0.5 * LOGIT_BIAS)
-        (weigh0, weigh1)[step % 2][:, lanes(n, CHUNK)] = pair.astype(BF16)
-
-    def fold(step, n):
-        acc[...] += jnp.dot(
-            (weigh0, weigh1)[step % 2][:, lanes(n, CHUNK)],
-            texts[pl.ds(pl.multiple_of(n * CHUNK, CHUNK), CHUNK), :],
-            preferred_element_type=F32,
-        )
-
-    def first_weights(n, carry):
-        weigh(0, n)
+        dst[...] = sigmoid_of(cosine).astype(BF16)
+
+    def fold(s, src):
+        rows, block = where(s)
+        acc[rows, :] += jnp.dot(src[...], texts[block, :], preferred_element_type=F32)
+
+    def two_parts(t, carry):
+        s = 2 * t
+        run_events(s + 1, range(1, 15, 2))
+        weigh(s + 1, weigh1)
+        fold(s, weigh0)
+        run_events(s + 2, range(2, 16, 2))
+        weigh(s + 2, weigh0)
+        fold(s + 1, weigh1)
         return carry
 
-    lax.fori_loop(0, TEXTS // CHUNK, first_weights, 0)
-    for step in range(4):
-        acc[...] = jnp.zeros_like(acc)
-
-        def part(n, carry, step=step):
-            if step < 3:
-                weigh(step + 1, n)
-            fold(step, n)
-            return carry
-
-        lax.fori_loop(0, TEXTS // CHUNK, part, 0)
-        if step == 0:
-            far = LOGIT_SCALE * acc[0:PAIRS, :]
-            unit = images[0:PAIRS, :].astype(F32)
-            pack(send_up.at[0, 0:64], far[0:64], unit[0:64])
-            pack(send_down.at[0, 0:64], far[64:128], unit[64:128])
-            grads_up[0].start()
-            grads_down[0].start()
-            unit = images[PAIRS:2 * PAIRS, :].astype(F32)
-            text = texts[0:PAIRS, :].astype(F32)
-            cosine = jnp.sum(unit * text, axis=1, keepdims=True)
-            sigmoid = 0.5 + 0.5 * jnp.tanh(0.5 * LOGIT_SCALE * cosine + 0.5 * LOGIT_BIAS)
-            change = (sigmoid - 1.0).astype(BF16).astype(F32) - sigmoid.astype(BF16).astype(F32)
-            own_grad[...] = LOGIT_SCALE * (acc[PAIRS:2 * PAIRS, :] + change * text)
-            for near, far_copy in zip(feats_near, feats_far):
-                near.wait_recv()
-                far_copy.start()
-            continue
-        for side, sends, recvs, grads in (
-            (0, send_up, recv_up, grads_up), (1, send_down, recv_down, grads_down)
-        ):
-            grads[step - 1].wait_recv()
-            first = (2 * step + side) * PAIRS
-            full = LOGIT_SCALE * acc[side * PAIRS:(side + 1) * PAIRS, :]
-            unit = images[first:first + PAIRS, :].astype(F32)
-            if step > 1:
-                pack(sends.at[step], full + unpack(recvs.at[step - 1], unit), unit)
-            else:
-                come = slice(64 * side, 64 * side + 64)
-                kept = slice(64 - 64 * side, 128 - 64 * side)
-                both = full[come] + unpack(recvs.at[0, 0:64], unit[come])
-                pack(sends.at[step, come], both, unit[come])
-                pack(sends.at[step, kept], full[kept], unit[kept])
-            grads[step].start()
-        if step == 1:
-            for copy in feats_far:
-                copy.wait_recv()
-            feats_cross.start()
+    weigh(jnp.int32(0), weigh0)
+    lax.fori_loop(0, 7, two_parts, 0)
+    for event in schedule[15]:
+        event()
+    weigh(jnp.int32(15), weigh1)
+    fold(jnp.int32(14), weigh0)
+    fold(jnp.int32(15), weigh1)
+    for hop in (2, 3):
+        give(hop, 0)
+        give(hop, 1)
+    unit = images[PAIRS:2 * PAIRS, :].astype(F32)
+    text = texts[0:PAIRS, :].astype(F32)
+    cosine = jnp.sum(unit * text, axis=1, keepdims=True)
+    sigmoid = sigmoid_of(cosine)
+    change = (sigmoid - 1.0).astype(BF16).astype(F32) - sigmoid.astype(BF16).astype(F32)
+    own_grad[...] = LOGIT_SCALE * (acc[PAIRS:2 * PAIRS, :] + change * text)
 
     state_out.wait()
     state_tile[...] = jnp.zeros_like(state_tile)
@@ -398,9 +436,12 @@
     users = lax.broadcasted_iota(jnp.int32, (PAIRS, USERS), 1).astype(F32)
     bound = jnp.sum(jnp.where(local_column == users, norms_ref[...], 0.0), axis=1, keepdims=True)
     unit = images[PAIRS:2 * PAIRS, :].astype(F32)
-    grads_up[3].wait_recv()
-    grads_down[3].wait_recv()
-    unit_grad = own_grad[...] + unpack(recv_up.at[3], unit) + unpack(recv_down.at[3], unit)
+    for late in range(2):
+        for side in sides:
+            side.copies[5 + late].wait_recv()
+            start, stop = side.rows[late]
+            own_grad[start:stop, :] += unpack(side.recvs.at[5 + late], unit[start:stop])
+    unit_grad = own_grad[...]
     inner = jnp.sum(raw * unit_grad, axis=1, keepdims=True)
     embed_grad = inverse * unit_grad - inverse * inverse * inverse * raw * inner
     grad_gram = lax.dot_general(
@@ -586,14 +627,14 @@
             pltpu.VMEM((TEXTS, E), BF16),
             pltpu.VMEM((Z * PAIRS, E), BF16),
             pltpu.VMEM((PAIRS, E), F32),
-            pltpu.VMEM((IMAGES, E), F32),
+            pltpu.VMEM((Z * PAIRS, E), F32),
             pltpu.VMEM((PAIRS, E), F32),
-            pltpu.VMEM((IMAGES, TEXTS), BF16),
-            pltpu.VMEM((IMAGES, TEXTS), BF16),
-            pltpu.VMEM((4, PAIRS, SLOT), BF16),
-            pltpu.VMEM((4, PAIRS, SLOT), BF16),
-            pltpu.VMEM((4, PAIRS, SLOT), BF16),
-            pltpu.VMEM((4, PAIRS, SLOT), BF16),
+            pltpu.VMEM((IMAGES, CHUNK), BF16),
+            pltpu.VMEM((IMAGES, CHUNK), BF16),
+            pltpu.VMEM((7, PAIRS // 2, SLOT), BF16),
+            pltpu.VMEM((7, PAIRS // 2, SLOT), BF16),
+            pltpu.VMEM((7, PAIRS // 2, SLOT), BF16),
+            pltpu.VMEM((7, PAIRS // 2, SLOT), BF16),
             pltpu.VMEM((W, 8 * PAIRS), BF16),
             pltpu.VMEM((PAIRS, E), BF16),
             pltpu.VMEM((8 * PAIRS, 128), BF16),

time: 142 us -> 147 us (1.035)
  Pallas kernels: 134 us -> 140 us
    pallas_call x1, Pallas kernels: 134 us -> 140 us  [body(): pl.pallas_call(kernel, out_shape=(jax.ShapeDtypeStruct((W, E), BF16), jax...]
where the time goes in v3:
time: 147 us; the launch traced here: 146 us
  Pallas kernels  140 us (95%)
  local copies, waits for them, and re-layouts  5.48 us (4%)
    pallas_call x1, Pallas kernels, body(): pl.pallas_call(kernel, out_shape=(jax.ShapeDtypeStruct((W, E), BF16), jax...  140 us
    unnamed x9, local copies, waits for them, and re-layouts  4.82 us

profile of v3, /device:TPU:1, one launch (start us, length us, event | category | flops | bytes accessed | tf_op | source)
XLA Modules:
  0.0 146.5 jit_solution(16189297458656127426)
XLA Ops:
  0.6 0.8 fusion.3
  1.5 0.0 copy-start
  1.5 1.0 copy-done
  2.5 0.0 copy-start.1
  2.5 0.9 copy-done.1
  3.4 0.0 copy-start.2
  3.4 0.7 copy-done.2
  4.1 0.0 copy-start.3
  4.1 0.7 copy-done.3
  4.8 139.5 %shard_map.95 = (bf16[1408,1024]{1,0:T(8,128)(2,1)S(1)}, f32[8,8,128]{2,1,0:T(8,128)S(1)}) custom-call(bf16[128,1408]{1,0:T(8,128)(2,1)S(1)} %copy-done, bf16[128,1024]{1,0:T(8,128)(2,1)S(1)} %copy-done.1, bf16[1408,1024]{1,0:T(8,128)(2,1)} %proj_hbm.1, f32[1,16]{1,0:T(1,128)S(1)} %bitcast.15, s32[1,128]{1,0:T(1,128)S(1)} %bitcast.16, ...), custom_call_target="tpu_custom_call" | custom-call | tf_op jit(solution)/shard_map/pallas_call | solution.py:612
  144.3 0.6 constant_dynamic-slice_fusion
  144.9 1.6 %copy.17 = bf16[1408,1024]{1,0:T(8,128)(2,1)} copy(bf16[1408,1024]{1,0:T(8,128)(2,1)S(1)} %get-tuple-element.8) | data formatting | bytes 5767168
  (4 shorter events, 0.0 us)
Async XLA Ops:
  1.5 1.0 copy-start
  2.5 0.9 copy-start.1
  3.4 0.7 copy-start.2
  4.1 0.7 copy-start.3

commit v4 on v2

--- a/solution.py
+++ b/solution.py
@@ -138,7 +138,7 @@
         load.start()
     loads[0].wait()
     text = text_ref[...].astype(F32)
-    texts[0:PAIRS, :] = (
+    texts[0, 0, 0] = (
         text * lax.rsqrt(jnp.sum(text * text, axis=1, keepdims=True) + EPSILON)
     ).astype(BF16)
 
@@ -152,73 +152,48 @@
     def lanes(index, width=128):
         return pl.ds(pl.multiple_of(index * width, width), width)
 
-    def slot(rx, ry, rows, core=0):
-        base = (core * 16 + rx * 4 + ry) * PAIRS
-        return texts.at[base + rows[0]:base + rows[1], :]
-
-    def hop(axis, up, rx, ry, rows):
+    low, high = (0, 64), (64, 128)
+
+    def unit_of(rx, ry, rows, core=0):
+        return texts.at[core, rx, ry, rows[0]:rows[1], :]
+
+    def along(axis, up, rx, ry, rows):
         step = 3 if up else 1
         if axis == "x":
-            return net.plan(slot(rx, ry, rows), slot((rx + step) % 4, ry, rows), x_up if up else x_down)
-        return net.plan(slot(rx, ry, rows), slot(rx, (ry + step) % 4, rows), y_up if up else y_down)
-
+            return net.plan(unit_of(rx, ry, rows), unit_of((rx + step) % 4, ry, rows), x_up if up else x_down)
+        return net.plan(unit_of(rx, ry, rows), unit_of(rx, (ry + step) % 4, rows), y_up if up else y_down)
+
+    every, front, back = slice(0, 4), slice(0, 2), slice(2, 4)
+    first = [
+        [along("x", up, 0, 0, low) for up in (True, False)],
+        [along("y", up, 0, 0, high) for up in (True, False)],
+    ]
+    first_far = [
+        [along("x", True, 3, 0, (0, 32)), along("x", False, 1, 0, (32, 64))],
+        [along("y", True, 0, 3, (64, 96)), along("y", False, 0, 1, (96, 128))],
+    ]
+    second = [
+        [along("y", up, every, 0, low) for up in (True, False)],
+        [along("x", up, 0, every, high) for up in (True, False)],
+    ]
+    second_far = [
+        [along("y", True, front, 3, low), along("y", False, back, 1, low)],
+        [along("x", True, 3, front, high), along("x", False, 1, back, high)],
+    ]
     crossings = []
 
     def cross(rx, ry, rows):
-        crossings.append(net.push(slot(rx, ry, rows), slot(rx, ry, rows, 1), across))
-
-    class Half:
-        def __init__(self, first, second, low):
-            self.rows, self.swap = (low, low + 64), first == "y"
-            self.parts = ((low, low + 32), (low + 32, low + 64))
-            r, p = self.rows, self.parts
-            self.first = [hop(first, up, 0, 0, r) for up in (True, False)]
-            self.relay = [hop(first, up, *self.at(3 if up else 1, 0), p[0 if up else 1]) for up in (True, False)]
-            self.second = [[hop(second, up, *self.at(a, 0), r) for up in (True, False)] for a in range(4)]
-            self.last = [
-                [hop(second, up, *self.at(a, 3 if up else 1), p[0 if up else 1]) for up in (True, False)]
-                for a in range(4)
-            ]
-
-        def at(self, a, b):
-            return (b, a) if self.swap else (a, b)
-
-        def open(self, a):
-            for copy in self.second[a]:
-                copy.start()
-
-        def got_first(self, i):
-            a = (3, 1)[i]
-            self.first[i].wait_recv()
-            self.relay[i].start()
-            self.open(a)
-            cross(*self.at(a, 0), self.rows)
-
-        def got_relay(self):
-            for copy in self.relay:
-                copy.wait_recv()
-            self.open(2)
-            cross(*self.at(2, 0), self.rows)
-
-        def got_second(self, a):
-            for i in range(2):
-                self.second[a][i].wait_recv()
-                self.last[a][i].start()
-                cross(*self.at(a, (3, 1)[i]), self.rows)
-
-        def got_last(self, a):
-            for copy in self.last[a]:
-                copy.wait_recv()
-            cross(*self.at(a, 2), self.rows)
-
-    low, high = Half("x", "y", 0), Half("y", "x", 64)
-    halves = (low, high)
-    for half in halves:
-        for copy in half.first:
+        crossings.append(net.push(unit_of(rx, ry, rows), unit_of(rx, ry, rows, 1), across))
+
+    def start(copies):
+        for copy in copies:
             copy.start()
-    for half in halves:
-        half.open(0)
-    cross(0, 0, (0, PAIRS))
+
+    def arrive(copies):
+        for copy in copies:
+            copy.wait_recv()
+
+    start(first[0] + first[1])
 
     for load in loads[1:]:
         load.wait()
@@ -253,31 +228,28 @@
         owner_slot,
     )
 
-    for half in halves:
-        half.got_first(0)
-        half.got_first(1)
-    for half in halves:
-        half.got_second(0)
+    for i in range(2):
+        for near, far in zip(first[i], first_far[i]):
+            near.wait_recv()
+            far.start()
+    for i in range(2):
+        arrive(first_far[i])
+        start(second[i])
+    cross(every, 0, low)
+    cross(0, every, high)
     turn(0)
-    for half in halves:
-        half.got_relay()
-    for half in halves:
-        half.got_last(0)
-    for a in (3, 1):
-        for half in halves:
-            half.got_second(a)
     turn(1)
-    for half in halves:
-        half.got_second(2)
-    for a in (3, 1):
-        for half in halves:
-            half.got_last(a)
+    for j in range(2):
+        for i in range(2):
+            second[i][j].wait_recv()
+            second_far[i][j].start()
+            at = 3 if j == 0 else 1
+            cross(*((every, at, low), (at, every, high))[i])
     turn(2)
-    for half in halves:
-        half.got_last(2)
+    for i in range(2):
+        arrive(second_far[i])
+        cross(*((every, 2, low), (2, every, high))[i])
     turn(3)
-    for copy in crossings:
-        copy.wait_recv()
 
     def feats_slot(ry, rows=(0, W)):
         return feats_all.at[rows[0]:rows[1], ry * PAIRS:(ry + 1) * PAIRS]
@@ -307,23 +279,27 @@
     def unpack(src, unit):
         return src[:, 0:E].astype(F32) + src[:, E:SLOT].astype(F32)[:, 0:1] * unit
 
+    def texts_of(core):
+        return texts[core].reshape(CHUNK, E)
+
     def weigh(step, n):
         rows = slice(step * IMAGES, (step + 1) * IMAGES)
         cosine = lax.dot_general(
-            images[rows, :], texts[pl.ds(pl.multiple_of(n * CHUNK, CHUNK), CHUNK), :],
-            (((1,), (1,)), ((), ())), preferred_element_type=F32,
+            images[rows, :], texts_of(n), (((1,), (1,)), ((), ())), preferred_element_type=F32
         )
         pair = 0.5 + 0.5 * jnp.tanh(0.5 * LOGIT_SCALE * cosine + 0.5 * LOGIT_BIAS)
         (weigh0, weigh1)[step % 2][:, lanes(n, CHUNK)] = pair.astype(BF16)
 
     def fold(step, n):
         acc[...] += jnp.dot(
-            (weigh0, weigh1)[step % 2][:, lanes(n, CHUNK)],
-            texts[pl.ds(pl.multiple_of(n * CHUNK, CHUNK), CHUNK), :],
-            preferred_element_type=F32,
+            (weigh0, weigh1)[step % 2][:, lanes(n, CHUNK)], texts_of(n), preferred_element_type=F32
         )
 
     def first_weights(n, carry):
+        @pl.when(n == 1)
+        def _():
+            arrive(crossings)
+
         weigh(0, n)
         return carry
 
@@ -346,7 +322,7 @@
             grads_up[0].start()
             grads_down[0].start()
             unit = images[PAIRS:2 * PAIRS, :].astype(F32)
-            text = texts[0:PAIRS, :].astype(F32)
+            text = texts[0, 0, 0].astype(F32)
             cosine = jnp.sum(unit * text, axis=1, keepdims=True)
             sigmoid = 0.5 + 0.5 * jnp.tanh(0.5 * LOGIT_SCALE * cosine + 0.5 * LOGIT_BIAS)
             change = (sigmoid - 1.0).astype(BF16).astype(F32) - sigmoid.astype(BF16).astype(F32)
@@ -493,66 +469,43 @@
         copy.wait_recv()
     whole = z_tiles[...].astype(F32)
     whole = jnp.concatenate([whole[piece * PADDED:piece * PADDED + BLOCK] for piece in range(Z)], axis=0)
-    share_rows = pl.ds(pl.multiple_of(x * SHARE, 16), SHARE)
-    weights_ref[share_rows, lanes(k)] = whole.astype(BF16)
-
-    half_rows = SHARE // 2
-
-    def part_rows(index, upper):
-        return pl.ds(pl.multiple_of(index * SHARE + upper * half_rows, 16), half_rows)
-
-    first = weights_ref.at[part_rows(x, 0), lanes(k)]
-    second = weights_ref.at[part_rows(x, 1), lanes(k)]
-    moves_y = [net.push(first, first, target) for target in at_y]
-    moves_x = [net.push(second, second, target) for target in at_x]
-    for copy in moves_y:
-        copy.wait_recv()
-    crossings = []
-
-    def give(piece):
-        crossings.append(net.push(piece, piece, across))
-
-    def low_piece(index, rows=(0, half_rows)):
-        start = pl.multiple_of(index * SHARE + rows[0], 16)
-        return weights_ref.at[pl.ds(start, rows[1] - rows[0]), lanes(c, 512)]
-
-    def high_piece(index, away):
-        return weights_ref.at[part_rows(shift(x, index, X), 1), lanes(c * 4 + shift(y, away, Y))]
-
-    low_moves = [net.push(low_piece(x), low_piece(x), target) for target in (x_up, x_down)]
-    give(low_piece(x))
-    for copy in moves_x:
-        copy.wait_recv()
-    high_moves = [
-        [net.push(high_piece(a, 0), high_piece(a, 0), target) for a in range(X)]
-        for target in (y_up, y_down)
-    ]
-    for a in range(X):
-        give(high_piece(a, 0))
-    low_relays, high_relays = [], []
+    weights_ref[x, :, lanes(k)] = whole.astype(BF16)
+
+    half = SHARE // 2
+
+    def low_piece(index, rows=(0, half)):
+        return weights_ref.at[index, rows[0]:rows[1], lanes(c, 512)]
+
+    def high_piece(away, shares=slice(0, X)):
+        return weights_ref.at[shares, half:SHARE, lanes(c * 4 + shift(y, away, Y))]
+
+    def send(piece, target):
+        return net.push(piece, piece, target)
+
+    moves_y = [send(weights_ref.at[x, 0:half, lanes(k)], target) for target in at_y]
+    moves_x = [send(weights_ref.at[x, half:SHARE, lanes(k)], target) for target in at_x]
+    arrive(moves_y)
+    low_moves = [send(low_piece(x), target) for target in (x_up, x_down)]
+    arrive(moves_x)
+    high_moves = [send(high_piece(0), target) for target in (y_up, y_down)]
+    given = [send(low_piece(x), across), send(high_piece(0), across)]
+    far = []
     for copy, away, rows_sent, target in (
-        (low_moves[0], 3, (0, 96), x_up), (low_moves[1], 1, (96, half_rows), x_down)
+        (low_moves[0], 3, (0, 96), x_up), (low_moves[1], 1, (96, half), x_down)
     ):
         copy.wait_recv()
         index = shift(x, away, X)
-        low_relays.append(net.push(low_piece(index, rows_sent), low_piece(index, rows_sent), target))
-        give(low_piece(index))
-    for copies, away, sent, target in ((high_moves[0], 3, (0, 1), y_up), (high_moves[1], 1, (2, 3), y_down)):
-        for copy in copies:
-            copy.wait_recv()
-        for a in sent:
-            high_relays.append(net.push(high_piece(a, away), high_piece(a, away), target))
-        for a in range(X):
-            give(high_piece(a, away))
-    for copy in low_relays:
+        far.append(send(low_piece(index, rows_sent), target))
+        given.append(send(low_piece(index), across))
+    for copy, away, shares, target in (
+        (high_moves[0], 3, slice(0, 2), y_up), (high_moves[1], 1, slice(2, 4), y_down)
+    ):
         copy.wait_recv()
-    give(low_piece(shift(x, 2, X)))
-    for copy in high_relays:
-        copy.wait_recv()
-    for a in range(X):
-        give(high_piece(a, 2))
-    for copy in crossings:
-        copy.wait_recv()
+        far.append(send(high_piece(away, shares), target))
+        given.append(send(high_piece(away), across))
+    arrive(far)
+    given += [send(low_piece(shift(x, 2, X)), across), send(high_piece(2), across)]
+    arrive(given)
     sums_out.wait()
     state_out.wait_sent()
     sums_out.wait_sent()
@@ -571,7 +524,7 @@
     weights, sums = pl.pallas_call(
         kernel,
         out_shape=(
-            jax.ShapeDtypeStruct((W, E), BF16),
+            jax.ShapeDtypeStruct((X, SHARE, E), BF16),
             jax.ShapeDtypeStruct((8, 8, 128), F32),
         ),
         in_specs=[pl.BlockSpec(memory_space=pl.ANY)] * 6,
@@ -583,7 +536,7 @@
             pltpu.VMEM((1, PAIRS), jnp.int32),
             pltpu.VMEM((8, 3, 8, 128), F32),
             pltpu.VMEM((W, E), BF16),
-            pltpu.VMEM((TEXTS, E), BF16),
+            pltpu.VMEM((2, X, Y, PAIRS, E), BF16),
             pltpu.VMEM((Z * PAIRS, E), BF16),
             pltpu.VMEM((PAIRS, E), F32),
             pltpu.VMEM((IMAGES, E), F32),
@@ -620,7 +573,7 @@
         user_ids.reshape(1, PAIRS), state,
     )
     sums = sums[:, :6].transpose(1, 0, 2).reshape(48, 128)
-    return weights, lax.dynamic_slice(sums, (4 * c, 0), (44, 128))
+    return weights.reshape(W, E), lax.dynamic_slice(sums, (4 * c, 0), (44, 128))
 
 
 def solution(mesh):

time: 142 us -> 145 us (1.021)
  Pallas kernels: 134 us -> 137 us
    pallas_call x1, Pallas kernels: 134 us -> 137 us  [body(): pl.pallas_call(kernel, out_shape=(jax.ShapeDtypeStruct((X, SHARE, E), BF1...]
where the time goes in v4:
time: 145 us; the launch traced here: 144 us
  Pallas kernels  137 us (94%)
  local copies, waits for them, and re-layouts  5.48 us (4%)
    pallas_call x1, Pallas kernels, body(): pl.pallas_call(kernel, out_shape=(jax.ShapeDtypeStruct((X, SHARE, E), BF1...  137 us
    unnamed x9, local copies, waits for them, and re-layouts  4.82 us

profile of v4, /device:TPU:1, one launch (start us, length us, event | category | flops | bytes accessed | tf_op | source)
XLA Modules:
  0.0 144.5 jit_solution(4202952344623278369)
XLA Ops:
  0.6 0.8 fusion.3
  1.5 0.0 copy-start
  1.5 1.0 copy-done
  2.5 0.0 copy-start.1
  2.5 0.9 copy-done.1
  3.4 0.0 copy-start.2
  3.4 0.7 copy-done.2
  4.1 0.0 copy-start.3
  4.1 0.7 copy-done.3
  4.8 137.5 %shard_map.95 = (bf16[4,352,1024]{2,1,0:T(8,128)(2,1)S(1)}, f32[8,8,128]{2,1,0:T(8,128)S(1)}) custom-call(bf16[128,1408]{1,0:T(8,128)(2,1)S(1)} %copy-done, bf16[128,1024]{1,0:T(8,128)(2,1)S(1)} %copy-done.1, bf16[1408,1024]{1,0:T(8,128)(2,1)} %proj_hbm.1, f32[1,16]{1,0:T(1,128)S(1)} %bitcast.17, s32[1,128]{1,0:T(1,128)S(1)} %bitcast.18, ...), custom_call_target="tpu_custom_call" | custom-call | tf_op jit(solution)/shard_map/pallas_call | solution.py:524
  142.3 0.6 constant_dynamic-slice_fusion
  142.9 1.6 %copy.17 = bf16[1408,1024]{1,0:T(8,128)(2,1)} copy(bf16[1408,1024]{1,0:T(8,128)(2,1)S(1)} %bitcast.16) | data formatting | bytes 5767168
  (4 shorter events, 0.0 us)
Async XLA Ops:
  1.5 1.0 copy-start
  2.5 0.9 copy-start.1
  3.4 0.7 copy-start.2
  4.1 0.7 copy-start.3

commit v5 on v3

--- a/solution.py
+++ b/solution.py
@@ -11,7 +11,6 @@
 LOGIT_BIAS = -5.0
 RATE = 0.5
 EPSILON = 1e-06
-LOG2_E = math.log2(math.e)
 
 MESH = pl.DeviceIdType.MESH
 X, Y, Z = 4, 4, 8
@@ -21,10 +20,10 @@
 PADDED = 48
 WIDE = Z * PADDED
 TEXTS = 2 * X * Y * PAIRS
-CHUNK = 512
-IMAGES = 4 * PAIRS
-SLOT = E + 128
-COPIES = 240
+CHUNK = 1024
+IMAGES = 2 * PAIRS
+HALF = PAIRS // 2
+COPIES = 256
 F32, BF16 = jnp.float32, jnp.bfloat16
 
 
@@ -33,11 +32,6 @@
     x, zh = lax.div(row, 4), lax.rem(row, 4)
     y, zl, c = lax.div(col, 4), lax.rem(lax.div(col, 2), 2), lax.rem(col, 2)
     return x, y, zh * 2 + zl, c
-
-
-def sigmoid_of(cosine):
-    power = cosine * (-LOGIT_SCALE * LOG2_E) + (-LOGIT_BIAS * LOG2_E)
-    return pl.reciprocal(1.0 + jnp.exp2(power), approx=True)
 
 
 def device(x, y, z, c):
@@ -114,8 +108,8 @@
     feats_hbm, text_hbm, proj_hbm, norms_hbm, ids_hbm, state_hbm,
     weights_ref, sums_ref,
     feats_ref, text_ref, norms_ref, ids_row, state_ref, proj, texts, images, raw_ref, acc, own_grad, weigh0, weigh1,
-    send_up, send_down, recv_up, recv_down,
-    feats_all, clipped, clipped_all, spread, x_send, x_recv, z_part, z_recv, z_tiles,
+    send_up, send_down, recv_up, recv_down, send_up_row, send_down_row, recv_up_row, recv_down_row,
+    feats_all, clipped, clipped_all, spread, x_send, x_recv, z_part, z_send, z_recv, z_tiles,
     state_recv, state_tile, sums_send, sq_send, sq_recv,
     load_sems, send_sems, recv_sems,
 ):
@@ -168,11 +162,10 @@
             return net.plan(slot(rx, ry, rows), slot((rx + step) % 4, ry, rows), x_up if up else x_down)
         return net.plan(slot(rx, ry, rows), slot(rx, (ry + step) % 4, rows), y_up if up else y_down)
 
-    crossings = [[] for _ in range(X)]
+    text_crossings = []
 
     def cross(rx, ry, rows):
-        crossings[rx].append(net.plan(slot(rx, ry, rows), slot(rx, ry, rows, 1), across))
-        return crossings[rx][-1]
+        text_crossings.append(net.push(slot(rx, ry, rows), slot(rx, ry, rows, 1), across))
 
     class Half:
         def __init__(self, first, second, low):
@@ -186,9 +179,6 @@
                 [hop(second, up, *self.at(a, 3 if up else 1), p[0 if up else 1]) for up in (True, False)]
                 for a in range(4)
             ]
-            self.cross = [
-                [cross(*self.at(a, b), r) if a or b else None for b in range(4)] for a in range(4)
-            ]
 
         def at(self, a, b):
             return (b, a) if self.swap else (a, b)
@@ -202,24 +192,28 @@
             self.first[i].wait_recv()
             self.relay[i].start()
             self.open(a)
-            self.cross[a][0].start()
+            cross(*self.at(a, 0), self.rows)
 
         def got_relay(self):
             for copy in self.relay:
                 copy.wait_recv()
             self.open(2)
-            self.cross[2][0].start()
+            cross(*self.at(2, 0), self.rows)
 
         def got_second(self, a):
             for i in range(2):
                 self.second[a][i].wait_recv()
                 self.last[a][i].start()
-                self.cross[a][(3, 1)[i]].start()
+                cross(*self.at(a, (3, 1)[i]), self.rows)
 
         def got_last(self, a):
             for copy in self.last[a]:
                 copy.wait_recv()
-            self.cross[a][2].start()
+            cross(*self.at(a, 2), self.rows)
+
+    def arrive(copies):
+        for copy in copies:
+            copy.wait_recv()
 
     low, high = Half("x", "y", 0), Half("y", "x", 64)
     halves = (low, high)
@@ -228,7 +222,7 @@
             copy.start()
     for half in halves:
         half.open(0)
-    cross(0, 0, (0, PAIRS)).start()
+    cross(0, 0, (0, PAIRS))
 
     for load in loads[1:]:
         load.wait()
@@ -279,15 +273,13 @@
     turn(1)
     for half in halves:
         half.got_second(2)
-    turn(2)
-
-    def got_last(a):
+    for a in (3, 1):
         for half in halves:
             half.got_last(a)
-
-    def got_cross(rx):
-        for copy in crossings[rx]:
-            copy.wait_recv()
+    turn(2)
+    for half in halves:
+        half.got_last(2)
+    turn(3)
 
     def feats_slot(ry, rows=(0, W)):
         return feats_all.at[rows[0]:rows[1], ry * PAIRS:(ry + 1) * PAIRS]
@@ -299,29 +291,49 @@
         net.plan(feats_slot(1, (W // 2, W)), feats_slot(2, (W // 2, W)), y_down),
     ]
     feats_cross = net.plan(feats_all.at[:, 0:512], feats_all.at[:, 512:1024], across)
+    def feats_open():
+        for copy in feats_near:
+            copy.start()
+
     def feats_on():
         for near, far in zip(feats_near, feats_far):
             near.wait_recv()
             far.start()
 
     def feats_over():
-        for copy in feats_far:
-            copy.wait_recv()
+        arrive(feats_far)
         feats_cross.start()
 
-    def pack(dst, full, unit):
-        along = jnp.sum(full * unit, axis=1, keepdims=True).astype(BF16).astype(F32)
-        dst[:, 0:E] = (full - along * unit).astype(BF16)
-        dst[:, E:SLOT] = jnp.broadcast_to(along, (full.shape[0], 128)).astype(BF16)
-
-    def unpack(src, unit):
-        return src[:, 0:E].astype(F32) + src[:, E:SLOT].astype(F32)[:, 0:1] * unit
+    pick = lax.broadcasted_iota(jnp.int32, (HALF, 128), 0) == lax.broadcasted_iota(
+        jnp.int32, (HALF, 128), 1
+    )
+
+    def pack(dst, dst_row, full, unit):
+        coefficient = jnp.sum(full * unit, axis=1, keepdims=True)
+        dst[...] = (full - coefficient * unit).astype(BF16)
+        row = jnp.sum(jnp.where(pick, coefficient, 0.0), axis=0, keepdims=True)
+        dst_row[...] = jnp.broadcast_to(row, (8, 128))
+
+    def unpack(src, src_row, unit):
+        coefficient = jnp.sum(jnp.where(pick, src_row[0:1, :], 0.0), axis=1, keepdims=True)
+        return src[...].astype(F32) + coefficient * unit
 
     class Side:
-        def __init__(self, first, come, sends, recvs, target):
+        def __init__(self, first, come, sends, recvs, send_rows, recv_rows, target):
             self.blocks, self.sends, self.recvs = (0, first, first + 2, first + 4), sends, recvs
+            self.send_rows, self.recv_rows = send_rows, recv_rows
             self.rows = ((64 - come, 128 - come), (come, come + 64))
-            self.copies = [net.plan(sends.at[i], recvs.at[i], target) for i in range(7)]
+            self.copies = [
+                (
+                    net.plan(sends.at[i], recvs.at[i], target),
+                    net.plan(send_rows.at[i], recv_rows.at[i], target),
+                )
+                for i in range(7)
+            ]
+
+        def take(self, i, unit):
+            arrive(self.copies[i])
+            return unpack(self.recvs.at[i], self.recv_rows.at[i], unit)
 
         def give(self, hop, late):
             i = 2 * hop - 1 + late
@@ -330,87 +342,71 @@
             unit = images[base + start:base + stop, :].astype(F32)
             full = LOGIT_SCALE * acc[base + start:base + stop, :]
             if hop > 1 or (hop == 1 and late):
-                come = i - 2
-                self.copies[come].wait_recv()
-                full = full + unpack(self.recvs.at[come], unit)
-            pack(self.sends.at[i], full, unit)
-            self.copies[i].start()
-
-    sides = (Side(2, 0, send_up, recv_up, z_up), Side(3, 64, send_down, recv_down, z_down))
+                full = full + self.take(i - 2, unit)
+            pack(self.sends.at[i], self.send_rows.at[i], full, unit)
+            for copy in self.copies[i]:
+                copy.start()
+
+    sides = (
+        Side(2, 0, send_up, recv_up, send_up_row, recv_up_row, z_up),
+        Side(3, 64, send_down, recv_down, send_down_row, recv_down_row, z_down),
+    )
 
     def give(hop, late):
         for side in sides:
             side.give(hop, late)
 
-    def open_sums():
-        give(0, 1)
-        give(1, 0)
-
     schedule = {
-        1: [lambda: got_last(3), lambda: got_last(1)],
-        3: [lambda: got_last(2)],
-        4: [lambda: turn(3), lambda: [copy.start() for copy in feats_near], state_out.start],
-        8: [lambda: got_cross(0), feats_on],
-        9: [lambda: got_cross(3)],
-        10: [lambda: got_cross(1)],
-        11: [lambda: got_cross(2)],
-        13: [open_sums, feats_over],
-        15: [lambda: give(1, 1)],
+        (0, 0): [feats_open, state_out.start],
+        (0, 2): [lambda: arrive(text_crossings)],
+        (1, 0): [lambda: give(0, 1)],
+        (1, 2): [feats_on],
+        (2, 0): [lambda: give(1, 0), lambda: give(1, 1)],
+        (2, 2): [feats_over],
+        (3, 0): [lambda: give(2, 0)],
+        (3, 1): [lambda: give(2, 1)],
     }
     acc[...] = jnp.zeros_like(acc)
 
-    def run_events(s, which):
-        for at in which:
-            if at in schedule:
-
-                @pl.when(s == at)
-                def _(events=schedule[at]):
-                    for event in events:
-                        event()
-
-    def where(s):
-        quarter, turn_at = lax.div(s, 4), lax.rem(s, 4)
-        near = jnp.logical_or(quarter == 0, quarter == 3)
-        rx = lax.select(turn_at == 0, 0, lax.select(turn_at == 1, 3, turn_at - 1))
-        rows = pl.ds(pl.multiple_of(lax.select(near, IMAGES, 0), IMAGES), IMAGES)
-        base = (lax.div(quarter, 2) * 4 + rx) * CHUNK
-        return rows, pl.ds(pl.multiple_of(base, CHUNK), CHUNK)
-
-    def weigh(s, dst):
-        rows, block = where(s)
-        cosine = lax.dot_general(
-            images[rows, :], texts[block, :], (((1,), (1,)), ((), ())), preferred_element_type=F32
-        )
-        dst[...] = sigmoid_of(cosine).astype(BF16)
-
-    def fold(s, src):
-        rows, block = where(s)
-        acc[rows, :] += jnp.dot(src[...], texts[block, :], preferred_element_type=F32)
-
-    def two_parts(t, carry):
-        s = 2 * t
-        run_events(s + 1, range(1, 15, 2))
-        weigh(s + 1, weigh1)
-        fold(s, weigh0)
-        run_events(s + 2, range(2, 16, 2))
-        weigh(s + 2, weigh0)
-        fold(s + 1, weigh1)
+    def grid_step(step, carry):
+        rows = pl.ds(pl.multiple_of(step * IMAGES, IMAGES), IMAGES)
+        buffers = (weigh0, weigh1)
+
+        def weigh(n):
+            cosine = lax.dot_general(
+                images[rows, :], texts[n * CHUNK:(n + 1) * CHUNK, :],
+                (((1,), (1,)), ((), ())), preferred_element_type=F32,
+            )
+            pair = 0.5 + 0.5 * jnp.tanh(0.5 * LOGIT_SCALE * cosine + 0.5 * LOGIT_BIAS)
+            buffers[n % 2][...] = pair.astype(BF16)
+
+        def fold(n):
+            acc[rows, :] += jnp.dot(
+                buffers[n % 2][...], texts[n * CHUNK:(n + 1) * CHUNK, :], preferred_element_type=F32
+            )
+
+        for n in range(TEXTS // CHUNK):
+            for (at, part), events in schedule.items():
+                if part == n:
+
+                    @pl.when(step == at)
+                    def _(events=events):
+                        for event in events:
+                            event()
+
+            weigh(n)
+            if n > 0:
+                fold(n - 1)
+        fold(TEXTS // CHUNK - 1)
         return carry
 
-    weigh(jnp.int32(0), weigh0)
-    lax.fori_loop(0, 7, two_parts, 0)
-    for event in schedule[15]:
-        event()
-    weigh(jnp.int32(15), weigh1)
-    fold(jnp.int32(14), weigh0)
-    fold(jnp.int32(15), weigh1)
-    for hop in (2, 3):
-        give(hop, 0)
-        give(hop, 1)
+    lax.fori_loop(0, 4, grid_step, 0)
+    give(3, 0)
+    give(3, 1)
     unit = images[PAIRS:2 * PAIRS, :].astype(F32)
     text = texts[0:PAIRS, :].astype(F32)
     cosine = jnp.sum(unit * text, axis=1, keepdims=True)
-    sigmoid = sigmoid_of(cosine)
+    sigmoid = 0.5 + 0.5 * jnp.tanh(0.5 * LOGIT_SCALE * cosine + 0.5 * LOGIT_BIAS)
     change = (sigmoid - 1.0).astype(BF16).astype(F32) - sigmoid.astype(BF16).astype(F32)
     own_grad[...] = LOGIT_SCALE * (acc[PAIRS:2 * PAIRS, :] + change * text)
 
@@ -438,9 +434,8 @@
     unit = images[PAIRS:2 * PAIRS, :].astype(F32)
     for late in range(2):
         for side in sides:
-            side.copies[5 + late].wait_recv()
             start, stop = side.rows[late]
-            own_grad[start:stop, :] += unpack(side.recvs.at[5 + late], unit[start:stop])
+            own_grad[start:stop, :] += side.take(5 + late, unit[start:stop])
     unit_grad = own_grad[...]
     inner = jnp.sum(raw * unit_grad, axis=1, keepdims=True)
     embed_grad = inverse * unit_grad - inverse * inverse * inverse * raw * inner
@@ -483,18 +478,19 @@
         moves[o - 1].wait_recv()
         total = total + x_recv[o - 1].astype(F32)
     z_part[...] = total
+    z_send[...] = total.astype(BF16)
 
     def rows(index):
         return pl.ds(pl.multiple_of(index * PADDED, 16), PADDED)
 
     moves = [
-        net.push(z_part.at[rows(shift(z, o, Z)), :], z_recv.at[o - 1], at_z[o - 1])
+        net.push(z_send.at[rows(shift(z, o, Z)), :], z_recv.at[o - 1], at_z[o - 1])
         for o in range(1, Z)
     ]
     grad = z_part[rows(z), :]
     for o in range(1, Z):
         moves[o - 1].wait_recv()
-        grad = grad + z_recv[o - 1]
+        grad = grad + z_recv[o - 1].astype(F32)
 
     new_sum = state_tile[0] + grad
     update = new_sum + state_tile[1]
@@ -534,66 +530,43 @@
         copy.wait_recv()
     whole = z_tiles[...].astype(F32)
     whole = jnp.concatenate([whole[piece * PADDED:piece * PADDED + BLOCK] for piece in range(Z)], axis=0)
-    share_rows = pl.ds(pl.multiple_of(x * SHARE, 16), SHARE)
-    weights_ref[share_rows, lanes(k)] = whole.astype(BF16)
-
-    half_rows = SHARE // 2
-
-    def part_rows(index, upper):
-        return pl.ds(pl.multiple_of(index * SHARE + upper * half_rows, 16), half_rows)
-
-    first = weights_ref.at[part_rows(x, 0), lanes(k)]
-    second = weights_ref.at[part_rows(x, 1), lanes(k)]
-    moves_y = [net.push(first, first, target) for target in at_y]
-    moves_x = [net.push(second, second, target) for target in at_x]
-    for copy in moves_y:
-        copy.wait_recv()
-    crossings = []
-
-    def give(piece):
-        crossings.append(net.push(piece, piece, across))
-
-    def low_piece(index, rows=(0, half_rows)):
-        start = pl.multiple_of(index * SHARE + rows[0], 16)
-        return weights_ref.at[pl.ds(start, rows[1] - rows[0]), lanes(c, 512)]
-
-    def high_piece(index, away):
-        return weights_ref.at[part_rows(shift(x, index, X), 1), lanes(c * 4 + shift(y, away, Y))]
-
-    low_moves = [net.push(low_piece(x), low_piece(x), target) for target in (x_up, x_down)]
-    give(low_piece(x))
-    for copy in moves_x:
-        copy.wait_recv()
-    high_moves = [
-        [net.push(high_piece(a, 0), high_piece(a, 0), target) for a in range(X)]
-        for target in (y_up, y_down)
-    ]
-    for a in range(X):
-        give(high_piece(a, 0))
-    low_relays, high_relays = [], []
+    weights_ref[x, :, lanes(k)] = whole.astype(BF16)
+
+    half = SHARE // 2
+
+    def low_piece(index, rows=(0, half)):
+        return weights_ref.at[index, rows[0]:rows[1], lanes(c, 512)]
+
+    def high_piece(away, shares=slice(0, X)):
+        return weights_ref.at[shares, half:SHARE, lanes(c * 4 + shift(y, away, Y))]
+
+    def send(piece, target):
+        return net.push(piece, piece, target)
+
+    moves_y = [send(weights_ref.at[x, 0:half, lanes(k)], target) for target in at_y]
+    moves_x = [send(weights_ref.at[x, half:SHARE, lanes(k)], target) for target in at_x]
+    arrive(moves_y)
+    low_moves = [send(low_piece(x), target) for target in (x_up, x_down)]
+    arrive(moves_x)
+    high_moves = [send(high_piece(0), target) for target in (y_up, y_down)]
+    given = [send(low_piece(x), across), send(high_piece(0), across)]
+    far = []
     for copy, away, rows_sent, target in (
-        (low_moves[0], 3, (0, 96), x_up), (low_moves[1], 1, (96, half_rows), x_down)
+        (low_moves[0], 3, (0, 96), x_up), (low_moves[1], 1, (96, half), x_down)
     ):
         copy.wait_recv()
         index = shift(x, away, X)
-        low_relays.append(net.push(low_piece(index, rows_sent), low_piece(index, rows_sent), target))
-        give(low_piece(index))
-    for copies, away, sent, target in ((high_moves[0], 3, (0, 1), y_up), (high_moves[1], 1, (2, 3), y_down)):
-        for copy in copies:
-            copy.wait_recv()
-        for a in sent:
-            high_relays.append(net.push(high_piece(a, away), high_piece(a, away), target))
-        for a in range(X):
-            give(high_piece(a, away))
-    for copy in low_relays:
+        far.append(send(low_piece(index, rows_sent), target))
+        given.append(send(low_piece(index), across))
+    for copy, away, shares, target in (
+        (high_moves[0], 3, slice(0, 2), y_up), (high_moves[1], 1, slice(2, 4), y_down)
+    ):
         copy.wait_recv()
-    give(low_piece(shift(x, 2, X)))
-    for copy in high_relays:
-        copy.wait_recv()
-    for a in range(X):
-        give(high_piece(a, 2))
-    for copy in crossings:
-        copy.wait_recv()
+        far.append(send(high_piece(away, shares), target))
+        given.append(send(high_piece(away), across))
+    arrive(far)
+    given += [send(low_piece(shift(x, 2, X)), across), send(high_piece(2), across)]
+    arrive(given)
     sums_out.wait()
     state_out.wait_sent()
     sums_out.wait_sent()
@@ -612,7 +585,7 @@
     weights, sums = pl.pallas_call(
         kernel,
         out_shape=(
-            jax.ShapeDtypeStruct((W, E), BF16),
+            jax.ShapeDtypeStruct((X, SHARE, E), BF16),
             jax.ShapeDtypeStruct((8, 8, 128), F32),
         ),
         in_specs=[pl.BlockSpec(memory_space=pl.ANY)] * 6,
@@ -631,10 +604,14 @@
             pltpu.VMEM((PAIRS, E), F32),
             pltpu.VMEM((IMAGES, CHUNK), BF16),
             pltpu.VMEM((IMAGES, CHUNK), BF16),
-            pltpu.VMEM((7, PAIRS // 2, SLOT), BF16),
-            pltpu.VMEM((7, PAIRS // 2, SLOT), BF16),
-            pltpu.VMEM((7, PAIRS // 2, SLOT), BF16),
-            pltpu.VMEM((7, PAIRS // 2, SLOT), BF16),
+            pltpu.VMEM((7, HALF, E), BF16),
+            pltpu.VMEM((7, HALF, E), BF16),
+            pltpu.VMEM((7, HALF, E), BF16),
+            pltpu.VMEM((7, HALF, E), BF16),
+            pltpu.VMEM((7, 8, 128), F32),
+            pltpu.VMEM((7, 8, 128), F32),
+            pltpu.VMEM((7, 8, 128), F32),
+            pltpu.VMEM((7, 8, 128), F32),
             pltpu.VMEM((W, 8 * PAIRS), BF16),
             pltpu.VMEM((PAIRS, E), BF16),
             pltpu.VMEM((8 * PAIRS, 128), BF16),
@@ -642,7 +619,8 @@
             pltpu.VMEM((X - 1, WIDE, 128), BF16),
             pltpu.VMEM((X - 1, WIDE, 128), BF16),
             pltpu.VMEM((WIDE, 128), F32),
-            pltpu.VMEM((Z - 1, PADDED, 128), F32),
+            pltpu.VMEM((WIDE, 128), BF16),
+            pltpu.VMEM((Z - 1, PADDED, 128), BF16),
             pltpu.VMEM((WIDE, 128), BF16),
             pltpu.VMEM((8, 3, 8, 128), F32),
             pltpu.VMEM((3, PADDED, 128), F32),
@@ -661,7 +639,7 @@
         user_ids.reshape(1, PAIRS), state,
     )
     sums = sums[:, :6].transpose(1, 0, 2).reshape(48, 128)
-    return weights, lax.dynamic_slice(sums, (4 * c, 0), (44, 128))
+    return weights.reshape(W, E), lax.dynamic_slice(sums, (4 * c, 0), (44, 128))
 
 
 def solution(mesh):

time: 147 us -> 136 us (0.925)
  Pallas kernels: 140 us -> 129 us
    pallas_call x1, Pallas kernels: 140 us -> 129 us  [body(): pl.pallas_call(kernel, out_shape=(jax.ShapeDtypeStruct((X, SHARE, E), BF1...]
where the time goes in v5:
time: 136 us
  Pallas kernels  129 us (95%)
  local copies, waits for them, and re-layouts  5.48 us (4%)
    pallas_call x1, Pallas kernels, body(): pl.pallas_call(kernel, out_shape=(jax.ShapeDtypeStruct((X, SHARE, E), BF1...  129 us
    unnamed x9, local copies, waits for them, and re-layouts  4.82 us

profile of v5, /device:TPU:1, one launch (start us, length us, event | category | flops | bytes accessed | tf_op | source)
XLA Modules:
  0.0 135.9 jit_solution(627565395869698942)
XLA Ops:
  0.6 0.8 fusion.3
  1.5 0.0 copy-start
  1.5 1.0 copy-done
  2.5 0.0 copy-start.1
  2.5 0.9 copy-done.1
  3.4 0.0 copy-start.2
  3.4 0.7 copy-done.2
  4.1 0.0 copy-start.3
  4.1 0.7 copy-done.3
  4.8 128.9 %shard_map.95 = (bf16[4,352,1024]{2,1,0:T(8,128)(2,1)S(1)}, f32[8,8,128]{2,1,0:T(8,128)S(1)}) custom-call(bf16[128,1408]{1,0:T(8,128)(2,1)S(1)} %copy-done, bf16[128,1024]{1,0:T(8,128)(2,1)S(1)} %copy-done.1, bf16[1408,1024]{1,0:T(8,128)(2,1)} %proj_hbm.1, f32[1,16]{1,0:T(1,128)S(1)} %bitcast.17, s32[1,128]{1,0:T(1,128)S(1)} %bitcast.18, ...), custom_call_target="tpu_custom_call" | custom-call | tf_op jit(solution)/shard_map/pallas_call | solution.py:585
  133.7 0.6 constant_dynamic-slice_fusion
  134.3 1.6 %copy.17 = bf16[1408,1024]{1,0:T(8,128)(2,1)} copy(bf16[1408,1024]{1,0:T(8,128)(2,1)S(1)} %bitcast.16) | data formatting | bytes 5767168
  (4 shorter events, 0.0 us)
Async XLA Ops:
  1.5 1.0 copy-start
  2.5 0.9 copy-start.1
  3.4 0.7 copy-start.2
  4.1 0.7 copy-start.3

commit v6 on v5

--- a/solution.py
+++ b/solution.py
@@ -109,7 +109,8 @@
     weights_ref, sums_ref,
     feats_ref, text_ref, norms_ref, ids_row, state_ref, proj, texts, images, raw_ref, acc, own_grad, weigh0, weigh1,
     send_up, send_down, recv_up, recv_down, send_up_row, send_down_row, recv_up_row, recv_down_row,
-    feats_all, clipped, clipped_all, spread, x_send, x_recv, z_part, z_send, z_recv, z_tiles,
+    feats_all, clipped, clipped_all, shares, shares_send, x_recv, x_part, x_send, x_recv_last,
+    z_recv, z_send, z_recv_last, z_tiles,
     state_recv, state_tile, sums_send, sq_send, sq_recv,
     load_sems, send_sems, recv_sems,
 ):
@@ -241,6 +242,23 @@
     up[0].start()
     down[0].start()
 
+    feats_all[:, 0:PAIRS] = feats_ref[...].T
+    acc[...] = jnp.zeros_like(acc)
+    shares[...] = jnp.zeros_like(shares)
+    feat_gram = lax.dot_general(
+        feats_ref[...], feats_ref[...], (((1,), (1,)), ((), ())), preferred_element_type=F32
+    )
+    local_row = (ids_row[...] - (lax.axis_index("row") * 16 + col) * USERS).astype(F32)
+    square_shape = (PAIRS, PAIRS)
+    diagonal = lax.broadcasted_iota(jnp.int32, square_shape, 0) == lax.broadcasted_iota(
+        jnp.int32, square_shape, 1
+    )
+    local_column = jnp.sum(jnp.where(diagonal, local_row, 0.0), axis=1, keepdims=True)
+    same_user = local_column == local_row
+    users = lax.broadcasted_iota(jnp.int32, (PAIRS, USERS), 1).astype(F32)
+    bound = jnp.sum(jnp.where(local_column == users, norms_ref[...], 0.0), axis=1, keepdims=True)
+    feat_gram = jnp.where(same_user, feat_gram, 0.0)
+
     def turn(step):
         for ring in (up, down):
             ring[step].wait_recv()
@@ -284,7 +302,6 @@
     def feats_slot(ry, rows=(0, W)):
         return feats_all.at[rows[0]:rows[1], ry * PAIRS:(ry + 1) * PAIRS]
 
-    feats_all[:, 0:PAIRS] = feats_ref[...].T
     feats_near = [net.plan(feats_slot(0), feats_slot(3), y_up), net.plan(feats_slot(0), feats_slot(1), y_down)]
     feats_far = [
         net.plan(feats_slot(3, (0, W // 2)), feats_slot(2, (0, W // 2)), y_up),
@@ -366,7 +383,6 @@
         (3, 0): [lambda: give(2, 0)],
         (3, 1): [lambda: give(2, 1)],
     }
-    acc[...] = jnp.zeros_like(acc)
 
     def grid_step(step, carry):
         rows = pl.ds(pl.multiple_of(step * IMAGES, IMAGES), IMAGES)
@@ -418,19 +434,6 @@
             state_tile[a, first:first + 6, :] += state_recv[piece, a, 0:6, :]
 
     raw = raw_ref[...]
-    inverse = lax.rsqrt(jnp.sum(raw * raw, axis=1, keepdims=True) + EPSILON)
-    feat_gram = lax.dot_general(
-        feats_ref[...], feats_ref[...], (((1,), (1,)), ((), ())), preferred_element_type=F32
-    )
-    local_row = (ids_row[...] - (lax.axis_index("row") * 16 + col) * USERS).astype(F32)
-    square_shape = (PAIRS, PAIRS)
-    diagonal = lax.broadcasted_iota(jnp.int32, square_shape, 0) == lax.broadcasted_iota(
-        jnp.int32, square_shape, 1
-    )
-    local_column = jnp.sum(jnp.where(diagonal, local_row, 0.0), axis=1, keepdims=True)
-    same_user = local_column == local_row
-    users = lax.broadcasted_iota(jnp.int32, (PAIRS, USERS), 1).astype(F32)
-    bound = jnp.sum(jnp.where(local_column == users, norms_ref[...], 0.0), axis=1, keepdims=True)
     unit = images[PAIRS:2 * PAIRS, :].astype(F32)
     for late in range(2):
         for side in sides:
@@ -443,7 +446,7 @@
         embed_grad, embed_grad, (((1,), (1,)), ((), ())),
         precision=lax.Precision.HIGHEST, preferred_element_type=F32,
     )
-    terms = jnp.sum(jnp.where(same_user, feat_gram * grad_gram, 0.0), axis=0, keepdims=True)
+    terms = jnp.sum(feat_gram * grad_gram, axis=0, keepdims=True)
     user_sq = jnp.sum(jnp.where(same_user, terms, 0.0), axis=1, keepdims=True)
     factor = bound / jnp.maximum(jnp.sqrt(user_sq), bound)
     clipped[...] = (factor * embed_grad).astype(BF16)
@@ -457,40 +460,49 @@
         parts.append(net.push(clipped.at[:, lanes(other * 4 + shift(y, o, Y))], rows_of(1, 4 - o), at_y_across[o - 1]))
     parts.append(net.push(clipped.at[:, lanes(other * 4 + y)], rows_of(1, 0), across))
     clipped_all[0:PAIRS, :] = clipped[:, lanes(k)]
-    spread[...] = jnp.zeros_like(spread)
     feats_cross.wait_recv()
     for copy in parts:
         copy.wait_recv()
 
-    def share(index):
-        block = feats_all[pl.ds(pl.multiple_of(index * SHARE, 16), SHARE), :]
+    def rows(index):
+        return pl.ds(pl.multiple_of(index * PADDED, 16), PADDED)
+
+    x_moves = []
+    for o in (1, 2, 3, 0):
+        block = feats_all[pl.ds(pl.multiple_of(shift(x, o, X) * SHARE, 16), SHARE), :]
         part = jnp.dot(block, clipped_all[...], preferred_element_type=F32)
         for piece in range(Z):
-            spread[piece * PADDED:piece * PADDED + BLOCK, :] = part[piece * BLOCK:(piece + 1) * BLOCK]
-        return spread[...]
-
-    moves = []
-    for o in range(1, X):
-        x_send[o - 1] = share(shift(x, o, X)).astype(BF16)
-        moves.append(net.push(x_send.at[o - 1], x_recv.at[o - 1], at_x[o - 1]))
-    total = share(x)
-    for o in range(1, X):
-        moves[o - 1].wait_recv()
-        total = total + x_recv[o - 1].astype(F32)
-    z_part[...] = total
-    z_send[...] = total.astype(BF16)
-
-    def rows(index):
-        return pl.ds(pl.multiple_of(index * PADDED, 16), PADDED)
-
-    moves = [
-        net.push(z_send.at[rows(shift(z, o, Z)), :], z_recv.at[o - 1], at_z[o - 1])
+            shares[o, piece, 0:BLOCK, :] = part[piece * BLOCK:(piece + 1) * BLOCK]
+        shares_send[o] = shares[o].astype(BF16)
+        if o:
+            x_moves.append(net.push(shares_send.at[o, :, 0:32, :], x_recv.at[o - 1], at_x[o - 1]))
+    z_moves = [
+        net.push(shares_send.at[:, shift(z, o, Z), 32:PADDED, :], z_recv.at[o - 1], at_z[o - 1])
         for o in range(1, Z)
     ]
-    grad = z_part[rows(z), :]
+    total = shares[0, :, 0:32, :]
+    for o in range(1, X):
+        x_moves[o - 1].wait_recv()
+        total = total + x_recv[o - 1].astype(F32)
+    x_part[...] = total
+    x_send[...] = total.astype(BF16)
+    x_moves = [
+        net.push(x_send.at[shift(z, o, Z)], x_recv_last.at[o - 1], at_z[o - 1]) for o in range(1, Z)
+    ]
+    total = shares[:, z, 32:PADDED, :]
     for o in range(1, Z):
-        moves[o - 1].wait_recv()
-        grad = grad + z_recv[o - 1].astype(F32)
+        z_moves[o - 1].wait_recv()
+        total = total + z_recv[o - 1].astype(F32)
+    z_send[...] = total.astype(BF16)
+    z_moves = [net.push(z_send.at[o], z_recv_last.at[o - 1], at_x[o - 1]) for o in range(1, X)]
+    upper, lower = x_part[z], total[0]
+    for o in range(1, X):
+        z_moves[o - 1].wait_recv()
+        lower = lower + z_recv_last[o - 1].astype(F32)
+    for o in range(1, Z):
+        x_moves[o - 1].wait_recv()
+        upper = upper + x_recv_last[o - 1].astype(F32)
+    grad = jnp.concatenate([upper, lower], axis=0)
 
     new_sum = state_tile[0] + grad
     update = new_sum + state_tile[1]
@@ -588,7 +600,7 @@
             jax.ShapeDtypeStruct((X, SHARE, E), BF16),
             jax.ShapeDtypeStruct((8, 8, 128), F32),
         ),
-        in_specs=[pl.BlockSpec(memory_space=pl.ANY)] * 6,
+        in_specs=[pl.BlockSpec(memory_space=pltpu.HBM)] * 6,
         out_specs=(vmem, vmem),
         scratch_shapes=[
             pltpu.VMEM((PAIRS, W), BF16),
@@ -615,12 +627,15 @@
             pltpu.VMEM((W, 8 * PAIRS), BF16),
             pltpu.VMEM((PAIRS, E), BF16),
             pltpu.VMEM((8 * PAIRS, 128), BF16),
-            pltpu.VMEM((WIDE, 128), F32),
-            pltpu.VMEM((X - 1, WIDE, 128), BF16),
-            pltpu.VMEM((X - 1, WIDE, 128), BF16),
-            pltpu.VMEM((WIDE, 128), F32),
-            pltpu.VMEM((WIDE, 128), BF16),
-            pltpu.VMEM((Z - 1, PADDED, 128), BF16),
+            pltpu.VMEM((X, Z, PADDED, 128), F32),
+            pltpu.VMEM((X, Z, PADDED, 128), BF16),
+            pltpu.VMEM((X - 1, Z, 32, 128), BF16),
+            pltpu.VMEM((Z, 32, 128), F32),
+            pltpu.VMEM((Z, 32, 128), BF16),
+            pltpu.VMEM((Z - 1, 32, 128), BF16),
+            pltpu.VMEM((Z - 1, X, 16, 128), BF16),
+            pltpu.VMEM((X, 16, 128), BF16),
+            pltpu.VMEM((X - 1, 16, 128), BF16),
             pltpu.VMEM((WIDE, 128), BF16),
             pltpu.VMEM((8, 3, 8, 128), F32),
             pltpu.VMEM((3, PADDED, 128), F32),

time: 136 us -> 135 us (level)
  no operation moved by 1% of the time
where the time goes in v6:
time: 135 us
  Pallas kernels  128 us (95%)
  local copies, waits for them, and re-layouts  5.48 us (4%)
    pallas_call x1, Pallas kernels, body(): pl.pallas_call(kernel, out_shape=(jax.ShapeDtypeStruct((X, SHARE, E), BF1...  128 us
    unnamed x9, local copies, waits for them, and re-layouts  4.82 us

profile of v6, /device:TPU:1, one launch (start us, length us, event | category | flops | bytes accessed | tf_op | source)
XLA Modules:
  0.0 134.8 jit_solution(14169696492456142000)
XLA Ops:
  0.6 0.8 fusion.3
  1.5 0.0 copy-start
  1.5 1.0 copy-done
  2.5 0.0 copy-start.1
  2.5 0.9 copy-done.1
  3.4 0.0 copy-start.2
  3.4 0.7 copy-done.2
  4.1 0.0 copy-start.3
  4.1 0.7 copy-done.3
  4.8 127.8 %shard_map.95 = (bf16[4,352,1024]{2,1,0:T(8,128)(2,1)S(1)}, f32[8,8,128]{2,1,0:T(8,128)S(1)}) custom-call(bf16[128,1408]{1,0:T(8,128)(2,1)S(1)} %copy-done, bf16[128,1024]{1,0:T(8,128)(2,1)S(1)} %copy-done.1, bf16[1408,1024]{1,0:T(8,128)(2,1)} %proj_hbm.1, f32[1,16]{1,0:T(1,128)S(1)} %bitcast.17, s32[1,128]{1,0:T(1,128)S(1)} %bitcast.18, ...), custom_call_target="tpu_custom_call" | custom-call | tf_op jit(solution)/shard_map/pallas_call | solution.py:597
  132.6 0.6 constant_dynamic-slice_fusion
  133.2 1.6 %copy.17 = bf16[1408,1024]{1,0:T(8,128)(2,1)} copy(bf16[1408,1024]{1,0:T(8,128)(2,1)S(1)} %bitcast.16) | data formatting | bytes 5767168
  (4 shorter events, 0.0 us)
Async XLA Ops:
  1.5 1.0 copy-start
  2.5 0.9 copy-start.1
  3.4 0.7 copy-start.2
  4.1 0.7 copy-start.3

commit v7 on v6

--- a/solution.py
+++ b/solution.py
@@ -40,6 +40,15 @@
 
 def shift(value, by, size):
     return lax.rem(value + by, size)
+
+
+def wide(ref, rows):
+    return jnp.concatenate([ref[block, rows, :] for block in range(ref.shape[0])], axis=1)
+
+
+def put(ref, rows, value):
+    for block in range(ref.shape[0]):
+        ref[block, rows, :] = value[:, block * 128:(block + 1) * 128]
 
 
 class Copies:
@@ -139,9 +148,8 @@
         load.start()
     loads[0].wait()
     text = text_ref[...].astype(F32)
-    texts[0:PAIRS, :] = (
-        text * lax.rsqrt(jnp.sum(text * text, axis=1, keepdims=True) + EPSILON)
-    ).astype(BF16)
+    text = text * lax.rsqrt(jnp.sum(text * text, axis=1, keepdims=True) + EPSILON)
+    put(texts, slice(0, PAIRS), text.astype(BF16))
 
     barrier = pltpu.get_barrier_semaphore()
     partners = at_x + at_y + at_z + [across] + at_y_across + at_flip
@@ -155,7 +163,7 @@
 
     def slot(rx, ry, rows, core=0):
         base = (core * 16 + rx * 4 + ry) * PAIRS
-        return texts.at[base + rows[0]:base + rows[1], :]
+        return texts.at[:, base + rows[0]:base + rows[1], :]
 
     def hop(axis, up, rx, ry, rows):
         step = 3 if up else 1
@@ -232,9 +240,10 @@
     inverse = lax.rsqrt(jnp.sum(raw * raw, axis=1, keepdims=True) + EPSILON)
 
     def image(index, rows=(0, PAIRS)):
-        return images.at[index * PAIRS + rows[0]:index * PAIRS + rows[1], :]
-
-    images[PAIRS:2 * PAIRS, :] = (raw * inverse).astype(BF16)
+        return images.at[:, index * PAIRS + rows[0]:index * PAIRS + rows[1], :]
+
+    own_rows = slice(PAIRS, 2 * PAIRS)
+    put(images, own_rows, (raw * inverse).astype(BF16))
     up = [net.plan(image(a), image(b), z_up) for a, b in ((1, 7), (7, 5), (5, 3))]
     down = [net.plan(image(a), image(b), z_down) for a, b in ((1, 6), (6, 4), (4, 2))]
     up.append(net.plan(image(3, (0, 64)), image(0, (0, 64)), z_up))
@@ -356,7 +365,7 @@
             i = 2 * hop - 1 + late
             base = self.blocks[hop] * PAIRS
             start, stop = self.rows[late]
-            unit = images[base + start:base + stop, :].astype(F32)
+            unit = wide(images, slice(base + start, base + stop)).astype(F32)
             full = LOGIT_SCALE * acc[base + start:base + stop, :]
             if hop > 1 or (hop == 1 and late):
                 full = full + self.take(i - 2, unit)
@@ -390,15 +399,16 @@
 
         def weigh(n):
             cosine = lax.dot_general(
-                images[rows, :], texts[n * CHUNK:(n + 1) * CHUNK, :],
+                wide(images, rows), wide(texts, slice(n * CHUNK, (n + 1) * CHUNK)),
                 (((1,), (1,)), ((), ())), preferred_element_type=F32,
             )
             pair = 0.5 + 0.5 * jnp.tanh(0.5 * LOGIT_SCALE * cosine + 0.5 * LOGIT_BIAS)
-            buffers[n % 2][...] = pair.astype(BF16)
+            put(buffers[n % 2], slice(None), pair.astype(BF16))
 
         def fold(n):
             acc[rows, :] += jnp.dot(
-                buffers[n % 2][...], texts[n * CHUNK:(n + 1) * CHUNK, :], preferred_element_type=F32
+                wide(buffers[n % 2], slice(None)), wide(texts, slice(n * CHUNK, (n + 1) * CHUNK)),
+                preferred_element_type=F32,
             )
 
         for n in range(TEXTS // CHUNK):
@@ -419,8 +429,8 @@
     lax.fori_loop(0, 4, grid_step, 0)
     give(3, 0)
     give(3, 1)
-    unit = images[PAIRS:2 * PAIRS, :].astype(F32)
-    text = texts[0:PAIRS, :].astype(F32)
+    unit = wide(images, own_rows).astype(F32)
+    text = wide(texts, slice(0, PAIRS)).astype(F32)
     cosine = jnp.sum(unit * text, axis=1, keepdims=True)
     sigmoid = 0.5 + 0.5 * jnp.tanh(0.5 * LOGIT_SCALE * cosine + 0.5 * LOGIT_BIAS)
     change = (sigmoid - 1.0).astype(BF16).astype(F32) - sigmoid.astype(BF16).astype(F32)
@@ -434,7 +444,7 @@
             state_tile[a, first:first + 6, :] += state_recv[piece, a, 0:6, :]
 
     raw = raw_ref[...]
-    unit = images[PAIRS:2 * PAIRS, :].astype(F32)
+    unit = wide(images, own_rows).astype(F32)
     for late in range(2):
         for side in sides:
             start, stop = side.rows[late]
@@ -609,13 +619,13 @@
             pltpu.VMEM((1, PAIRS), jnp.int32),
             pltpu.VMEM((8, 3, 8, 128), F32),
             pltpu.VMEM((W, E), BF16),
-            pltpu.VMEM((TEXTS, E), BF16),
-            pltpu.VMEM((Z * PAIRS, E), BF16),
+            pltpu.VMEM((E // 128, TEXTS, 128), BF16),
+            pltpu.VMEM((E // 128, Z * PAIRS, 128), BF16),
             pltpu.VMEM((PAIRS, E), F32),
             pltpu.VMEM((Z * PAIRS, E), F32),
             pltpu.VMEM((PAIRS, E), F32),
-            pltpu.VMEM((IMAGES, CHUNK), BF16),
-            pltpu.VMEM((IMAGES, CHUNK), BF16),
+            pltpu.VMEM((CHUNK // 128, IMAGES, 128), BF16),
+            pltpu.VMEM((CHUNK // 128, IMAGES, 128), BF16),
             pltpu.VMEM((7, HALF, E), BF16),
             pltpu.VMEM((7, HALF, E), BF16),
             pltpu.VMEM((7, HALF, E), BF16),

time: 135 us -> 135 us (level)
  no operation moved by 1% of the time
where the time goes in v7:
time: 135 us
  Pallas kernels  128 us (95%)
  local copies, waits for them, and re-layouts  5.48 us (4%)
    pallas_call x1, Pallas kernels, body(): pl.pallas_call(kernel, out_shape=(jax.ShapeDtypeStruct((X, SHARE, E), BF1...  128 us
    unnamed x9, local copies, waits for them, and re-layouts  4.82 us

profile of v7, /device:TPU:1, one launch (start us, length us, event | category | flops | bytes accessed | tf_op | source)
XLA Modules:
  0.0 134.5 jit_solution(4515234898053463559)
XLA Ops:
  0.6 0.8 fusion.3
  1.5 0.0 copy-start
  1.5 1.0 copy-done
  2.5 0.0 copy-start.1
  2.5 0.9 copy-done.1
  3.4 0.0 copy-start.2
  3.4 0.7 copy-done.2
  4.1 0.0 copy-start.3
  4.1 0.7 copy-done.3
  4.8 127.6 %shard_map.95 = (bf16[4,352,1024]{2,1,0:T(8,128)(2,1)S(1)}, f32[8,8,128]{2,1,0:T(8,128)S(1)}) custom-call(bf16[128,1408]{1,0:T(8,128)(2,1)S(1)} %copy-done, bf16[128,1024]{1,0:T(8,128)(2,1)S(1)} %copy-done.1, bf16[1408,1024]{1,0:T(8,128)(2,1)} %proj_hbm.1, f32[1,16]{1,0:T(1,128)S(1)} %bitcast.17, s32[1,128]{1,0:T(1,128)S(1)} %bitcast.18, ...), custom_call_target="tpu_custom_call" | custom-call | tf_op jit(solution)/shard_map/pallas_call | solution.py:607
  132.3 0.6 constant_dynamic-slice_fusion
  133.0 1.6 %copy.17 = bf16[1408,1024]{1,0:T(8,128)(2,1)} copy(bf16[1408,1024]{1,0:T(8,128)(2,1)S(1)} %bitcast.16) | data formatting | bytes 5767168
  (4 shorter events, 0.0 us)
Async XLA Ops:
  1.5 1.0 copy-start
  2.5 0.9 copy-start.1
  3.4 0.7 copy-start.2
  4.1 0.7 copy-start.3

commit v8 on v6

--- a/solution.py
+++ b/solution.py
@@ -373,10 +373,38 @@
         for side in sides:
             side.give(hop, late)
 
+    buffers = (weigh0, weigh1)
+
+    def grid_step(rows, count, events):
+        def weigh(n):
+            cosine = lax.dot_general(
+                images[rows, :], texts[n * CHUNK:(n + 1) * CHUNK, :],
+                (((1,), (1,)), ((), ())), preferred_element_type=F32,
+            )
+            pair = 0.5 + 0.5 * jnp.tanh(0.5 * LOGIT_SCALE * cosine + 0.5 * LOGIT_BIAS)
+            buffers[n % 2][0:count, :] = pair.astype(BF16)
+
+        def fold(n):
+            acc[rows, :] += jnp.dot(
+                buffers[n % 2][0:count, :], texts[n * CHUNK:(n + 1) * CHUNK, :],
+                preferred_element_type=F32,
+            )
+
+        for n in range(TEXTS // CHUNK):
+            events(n)
+            weigh(n)
+            if n > 0:
+                fold(n - 1)
+        fold(TEXTS // CHUNK - 1)
+
+    def open_events(n):
+        if n == 0:
+            feats_open()
+            state_out.start()
+        if n == 2:
+            arrive(text_crossings)
+
     schedule = {
-        (0, 0): [feats_open, state_out.start],
-        (0, 2): [lambda: arrive(text_crossings)],
-        (1, 0): [lambda: give(0, 1)],
         (1, 2): [feats_on],
         (2, 0): [lambda: give(1, 0), lambda: give(1, 1)],
         (2, 2): [feats_over],
@@ -384,41 +412,25 @@
         (3, 1): [lambda: give(2, 1)],
     }
 
-    def grid_step(step, carry):
-        rows = pl.ds(pl.multiple_of(step * IMAGES, IMAGES), IMAGES)
-        buffers = (weigh0, weigh1)
-
-        def weigh(n):
-            cosine = lax.dot_general(
-                images[rows, :], texts[n * CHUNK:(n + 1) * CHUNK, :],
-                (((1,), (1,)), ((), ())), preferred_element_type=F32,
-            )
-            pair = 0.5 + 0.5 * jnp.tanh(0.5 * LOGIT_SCALE * cosine + 0.5 * LOGIT_BIAS)
-            buffers[n % 2][...] = pair.astype(BF16)
-
-        def fold(n):
-            acc[rows, :] += jnp.dot(
-                buffers[n % 2][...], texts[n * CHUNK:(n + 1) * CHUNK, :], preferred_element_type=F32
-            )
-
-        for n in range(TEXTS // CHUNK):
-            for (at, part), events in schedule.items():
+    def pair_step(step, carry):
+        def events(n):
+            for (at, part), todo in schedule.items():
                 if part == n:
 
                     @pl.when(step == at)
-                    def _(events=events):
-                        for event in events:
+                    def _(todo=todo):
+                        for event in todo:
                             event()
 
-            weigh(n)
-            if n > 0:
-                fold(n - 1)
-        fold(TEXTS // CHUNK - 1)
+        grid_step(pl.ds(pl.multiple_of(step * IMAGES, IMAGES), IMAGES), IMAGES, events)
         return carry
 
-    lax.fori_loop(0, 4, grid_step, 0)
+    grid_step(slice(0, PAIRS), PAIRS, open_events)
+    give(0, 1)
+    lax.fori_loop(1, 4, pair_step, 0)
     give(3, 0)
     give(3, 1)
+    grid_step(slice(PAIRS, 2 * PAIRS), PAIRS, lambda n: None)
     unit = images[PAIRS:2 * PAIRS, :].astype(F32)
     text = texts[0:PAIRS, :].astype(F32)
     cosine = jnp.sum(unit * text, axis=1, keepdims=True)

time: 135 us -> 135 us (level)
  no operation moved by 1% of the time
where the time goes in v8:
time: 135 us
  Pallas kernels  128 us (95%)
  local copies, waits for them, and re-layouts  5.48 us (4%)
    pallas_call x1, Pallas kernels, body(): pl.pallas_call(kernel, out_shape=(jax.ShapeDtypeStruct((X, SHARE, E), BF1...  128 us
    unnamed x9, local copies, waits for them, and re-layouts  4.82 us

profile of v8, /device:TPU:1, one launch (start us, length us, event | category | flops | bytes accessed | tf_op | source)
XLA Modules:
  0.0 134.7 jit_solution(3860920038115588921)
XLA Ops:
  0.6 0.8 fusion.3
  1.5 0.0 copy-start
  1.5 1.0 copy-done
  2.5 0.0 copy-start.1
  2.5 0.9 copy-done.1
  3.4 0.0 copy-start.2
  3.4 0.7 copy-done.2
  4.1 0.0 copy-start.3
  4.1 0.7 copy-done.3
  4.8 127.7 %shard_map.95 = (bf16[4,352,1024]{2,1,0:T(8,128)(2,1)S(1)}, f32[8,8,128]{2,1,0:T(8,128)S(1)}) custom-call(bf16[128,1408]{1,0:T(8,128)(2,1)S(1)} %copy-done, bf16[128,1024]{1,0:T(8,128)(2,1)S(1)} %copy-done.1, bf16[1408,1024]{1,0:T(8,128)(2,1)} %proj_hbm.1, f32[1,16]{1,0:T(1,128)S(1)} %bitcast.17, s32[1,128]{1,0:T(1,128)S(1)} %bitcast.18, ...), custom_call_target="tpu_custom_call" | custom-call | tf_op jit(solution)/shard_map/pallas_call | solution.py:609
  132.5 0.6 constant_dynamic-slice_fusion
  133.1 1.6 %copy.17 = bf16[1408,1024]{1,0:T(8,128)(2,1)} copy(bf16[1408,1024]{1,0:T(8,128)(2,1)S(1)} %bitcast.16) | data formatting | bytes 5767168
  (4 shorter events, 0.0 us)
Async XLA Ops:
  1.5 1.0 copy-start
  2.5 0.9 copy-start.1
  3.4 0.7 copy-start.2
  4.1 0.7 copy-start.3

commit v9 on v8

--- a/solution.py
+++ b/solution.py
@@ -131,18 +131,12 @@
     loads = [
         pltpu.make_async_copy(src, dst, load_sems.at[i])
         for i, (src, dst) in enumerate((
-            (text_hbm, text_ref), (feats_hbm, feats_ref), (proj_hbm, proj),
+            (feats_hbm, feats_ref), (proj_hbm, proj), (text_hbm, text_ref),
             (state_hbm, state_ref), (norms_hbm, norms_ref), (ids_hbm, ids_row),
         ))
     ]
     for load in loads:
         load.start()
-    loads[0].wait()
-    text = text_ref[...].astype(F32)
-    texts[0:PAIRS, :] = (
-        text * lax.rsqrt(jnp.sum(text * text, axis=1, keepdims=True) + EPSILON)
-    ).astype(BF16)
-
     barrier = pltpu.get_barrier_semaphore()
     partners = at_x + at_y + at_z + [across] + at_y_across + at_flip
     for target in partners:
@@ -152,6 +146,40 @@
 
     def lanes(index, width=128):
         return pl.ds(pl.multiple_of(index * width, width), width)
+
+    for load in loads[:2]:
+        load.wait()
+    raw = jnp.dot(feats_ref[...], proj[...], preferred_element_type=F32)
+    raw_ref[...] = raw
+    inverse = lax.rsqrt(jnp.sum(raw * raw, axis=1, keepdims=True) + EPSILON)
+    images[PAIRS:2 * PAIRS, :] = (raw * inverse).astype(BF16)
+
+    def image_hop(source, target_slot, half, target):
+        def rows_at(index):
+            return images.at[index * PAIRS + half * HALF:index * PAIRS + (half + 1) * HALF, :]
+
+        return net.plan(rows_at(source), rows_at(target_slot), target)
+
+    up = [[image_hop(a, b, half, z_up) for half in (0, 1)] for a, b in ((1, 7), (7, 5), (5, 3))]
+    down = [[image_hop(a, b, half, z_down) for half in (1, 0)] for a, b in ((1, 6), (6, 4), (4, 2))]
+    up.append([image_hop(3, 0, 0, z_up)])
+    down.append([image_hop(2, 0, 1, z_down)])
+    for part in range(2):
+        up[0][part].start()
+        down[0][part].start()
+
+    def turn(step, part):
+        for ring in (up, down):
+            ring[step][part].wait_recv()
+            if part < len(ring[min(step + 1, 3)]) and step < 3:
+                ring[step + 1][part].start()
+
+    for load in loads[2:]:
+        load.wait()
+    text = text_ref[...].astype(F32)
+    texts[0:PAIRS, :] = (
+        text * lax.rsqrt(jnp.sum(text * text, axis=1, keepdims=True) + EPSILON)
+    ).astype(BF16)
 
     def slot(rx, ry, rows, core=0):
         base = (core * 16 + rx * 4 + ry) * PAIRS
@@ -225,23 +253,6 @@
         half.open(0)
     cross(0, 0, (0, PAIRS))
 
-    for load in loads[1:]:
-        load.wait()
-    raw = jnp.dot(feats_ref[...], proj[...], preferred_element_type=F32)
-    raw_ref[...] = raw
-    inverse = lax.rsqrt(jnp.sum(raw * raw, axis=1, keepdims=True) + EPSILON)
-
-    def image(index, rows=(0, PAIRS)):
-        return images.at[index * PAIRS + rows[0]:index * PAIRS + rows[1], :]
-
-    images[PAIRS:2 * PAIRS, :] = (raw * inverse).astype(BF16)
-    up = [net.plan(image(a), image(b), z_up) for a, b in ((1, 7), (7, 5), (5, 3))]
-    down = [net.plan(image(a), image(b), z_down) for a, b in ((1, 6), (6, 4), (4, 2))]
-    up.append(net.plan(image(3, (0, 64)), image(0, (0, 64)), z_up))
-    down.append(net.plan(image(2, (64, 128)), image(0, (64, 128)), z_down))
-    up[0].start()
-    down[0].start()
-
     feats_all[:, 0:PAIRS] = feats_ref[...].T
     acc[...] = jnp.zeros_like(acc)
     shares[...] = jnp.zeros_like(shares)
@@ -258,12 +269,6 @@
     users = lax.broadcasted_iota(jnp.int32, (PAIRS, USERS), 1).astype(F32)
     bound = jnp.sum(jnp.where(local_column == users, norms_ref[...], 0.0), axis=1, keepdims=True)
     feat_gram = jnp.where(same_user, feat_gram, 0.0)
-
-    def turn(step):
-        for ring in (up, down):
-            ring[step].wait_recv()
-            if step < 3:
-                ring[step + 1].start()
 
     owner_slot = (lax.rem(y, 2) * 2 + zl) * 2 + c
     zh2 = z - zl
@@ -275,29 +280,28 @@
         owner_slot,
     )
 
-    for half in halves:
-        half.got_first(0)
-        half.got_first(1)
-    for half in halves:
-        half.got_second(0)
-    turn(0)
+    def both(event, at):
+        for half in halves:
+            event(half, at)
+
+    both(Half.got_first, 0)
+    turn(0, 0)
+    both(Half.got_first, 1)
+    turn(0, 1)
+    both(Half.got_second, 0)
     for half in halves:
         half.got_relay()
-    for half in halves:
-        half.got_last(0)
-    for a in (3, 1):
-        for half in halves:
-            half.got_second(a)
-    turn(1)
-    for half in halves:
-        half.got_second(2)
-    for a in (3, 1):
-        for half in halves:
-            half.got_last(a)
-    turn(2)
-    for half in halves:
-        half.got_last(2)
-    turn(3)
+    turn(1, 0)
+    both(Half.got_last, 0)
+    both(Half.got_second, 3)
+    turn(1, 1)
+    both(Half.got_second, 1)
+    turn(2, 0)
+    both(Half.got_second, 2)
+    both(Half.got_last, 3)
+    both(Half.got_last, 1)
+    turn(2, 1)
+    both(Half.got_last, 2)
 
     def feats_slot(ry, rows=(0, W)):
         return feats_all.at[rows[0]:rows[1], ry * PAIRS:(ry + 1) * PAIRS]
@@ -405,11 +409,10 @@
             arrive(text_crossings)
 
     schedule = {
-        (1, 2): [feats_on],
         (2, 0): [lambda: give(1, 0), lambda: give(1, 1)],
-        (2, 2): [feats_over],
+        (2, 1): [feats_on],
         (3, 0): [lambda: give(2, 0)],
-        (3, 1): [lambda: give(2, 1)],
+        (3, 2): [lambda: give(2, 1), feats_over],
     }
 
     def pair_step(step, carry):
@@ -425,12 +428,13 @@
         grid_step(pl.ds(pl.multiple_of(step * IMAGES, IMAGES), IMAGES), IMAGES, events)
         return carry
 
-    grid_step(slice(0, PAIRS), PAIRS, open_events)
+    grid_step(slice(PAIRS, 2 * PAIRS), PAIRS, open_events)
+    turn(3, 0)
+    grid_step(slice(0, PAIRS), PAIRS, lambda n: None)
     give(0, 1)
     lax.fori_loop(1, 4, pair_step, 0)
     give(3, 0)
     give(3, 1)
-    grid_step(slice(PAIRS, 2 * PAIRS), PAIRS, lambda n: None)
     unit = images[PAIRS:2 * PAIRS, :].astype(F32)
     text = texts[0:PAIRS, :].astype(F32)
     cosine = jnp.sum(unit * text, axis=1, keepdims=True)

time: 135 us -> 135 us (level)
  no operation moved by 1% of the time
where the time goes in v9:
time: 135 us
  Pallas kernels  128 us (95%)
  local copies, waits for them, and re-layouts  5.48 us (4%)
    pallas_call x1, Pallas kernels, body(): pl.pallas_call(kernel, out_shape=(jax.ShapeDtypeStruct((X, SHARE, E), BF1...  128 us
    unnamed x9, local copies, waits for them, and re-layouts  4.82 us

profile of v9, /device:TPU:1, one launch (start us, length us, event | category | flops | bytes accessed | tf_op | source)
XLA Modules:
  0.0 134.8 jit_solution(17732648907851973952)
XLA Ops:
  0.6 0.8 fusion.3
  1.5 0.0 copy-start
  1.5 1.0 copy-done
  2.5 0.0 copy-start.1
  2.5 0.9 copy-done.1
  3.4 0.0 copy-start.2
  3.4 0.7 copy-done.2
  4.1 0.0 copy-start.3
  4.1 0.7 copy-done.3
  4.8 127.8 %shard_map.95 = (bf16[4,352,1024]{2,1,0:T(8,128)(2,1)S(1)}, f32[8,8,128]{2,1,0:T(8,128)S(1)}) custom-call(bf16[128,1408]{1,0:T(8,128)(2,1)S(1)} %copy-done, bf16[128,1024]{1,0:T(8,128)(2,1)S(1)} %copy-done.1, bf16[1408,1024]{1,0:T(8,128)(2,1)} %proj_hbm.1, f32[1,16]{1,0:T(1,128)S(1)} %bitcast.17, s32[1,128]{1,0:T(1,128)S(1)} %bitcast.18, ...), custom_call_target="tpu_custom_call" | custom-call | tf_op jit(solution)/shard_map/pallas_call | solution.py:613
  132.6 0.6 constant_dynamic-slice_fusion
  133.3 1.6 %copy.17 = bf16[1408,1024]{1,0:T(8,128)(2,1)} copy(bf16[1408,1024]{1,0:T(8,128)(2,1)S(1)} %bitcast.16) | data formatting | bytes 5767168
  (4 shorter events, 0.0 us)
Async XLA Ops:
  1.5 1.0 copy-start
  2.5 0.9 copy-start.1
  3.4 0.7 copy-start.2
  4.1 0.7 copy-start.3

commit v10 on v9

--- a/solution.py
+++ b/solution.py
@@ -105,12 +105,12 @@
 
 
 def kernel(
-    feats_hbm, text_hbm, proj_hbm, norms_hbm, ids_hbm, state_hbm,
+    feats_hbm, text_hbm, proj_hbm, state_hbm,
     weights_ref, sums_ref,
-    feats_ref, text_ref, norms_ref, ids_row, state_ref, proj, texts, images, raw_ref, acc, own_grad, weigh0, weigh1,
+    feats_ref, text_ref, state_ref, proj, texts, images, raw_ref, acc, own_grad, weigh0, weigh1,
     send_up, send_down, recv_up, recv_down, send_up_row, send_down_row, recv_up_row, recv_down_row,
     feats_all, clipped, clipped_all, shares, shares_send, x_recv, x_part, x_send, x_recv_last,
-    z_recv, z_send, z_recv_last, z_tiles,
+    z_recv, z_send, z_recv_last, start_all, update_all,
     state_recv, state_tile, sums_send, sq_send, sq_recv,
     load_sems, send_sems, recv_sems,
 ):
@@ -132,7 +132,7 @@
         pltpu.make_async_copy(src, dst, load_sems.at[i])
         for i, (src, dst) in enumerate((
             (feats_hbm, feats_ref), (proj_hbm, proj), (text_hbm, text_ref),
-            (state_hbm, state_ref), (norms_hbm, norms_ref), (ids_hbm, ids_row),
+            (state_hbm, state_ref),
         ))
     ]
     for load in loads:
@@ -259,7 +259,7 @@
     feat_gram = lax.dot_general(
         feats_ref[...], feats_ref[...], (((1,), (1,)), ((), ())), preferred_element_type=F32
     )
-    local_row = (ids_row[...] - (lax.axis_index("row") * 16 + col) * USERS).astype(F32)
+    local_row = state_ref[0, 0, 6:7, :] - ((lax.axis_index("row") * 16 + col) * USERS).astype(F32)
     square_shape = (PAIRS, PAIRS)
     diagonal = lax.broadcasted_iota(jnp.int32, square_shape, 0) == lax.broadcasted_iota(
         jnp.int32, square_shape, 1
@@ -267,7 +267,7 @@
     local_column = jnp.sum(jnp.where(diagonal, local_row, 0.0), axis=1, keepdims=True)
     same_user = local_column == local_row
     users = lax.broadcasted_iota(jnp.int32, (PAIRS, USERS), 1).astype(F32)
-    bound = jnp.sum(jnp.where(local_column == users, norms_ref[...], 0.0), axis=1, keepdims=True)
+    bound = jnp.sum(jnp.where(local_column == users, state_ref[0, 0, 7:8, 0:USERS], 0.0), axis=1, keepdims=True)
     feat_gram = jnp.where(same_user, feat_gram, 0.0)
 
     owner_slot = (lax.rem(y, 2) * 2 + zl) * 2 + c
@@ -449,6 +449,12 @@
         for a in range(3):
             state_tile[a, first:first + 6, :] += state_recv[piece, a, 0:6, :]
 
+    def rows(index):
+        return pl.ds(pl.multiple_of(index * PADDED, 16), PADDED)
+
+    start_all[rows(z), :] = state_tile[2]
+    start_moves = [net.push(start_all.at[rows(z), :], start_all.at[rows(z), :], target) for target in at_z]
+
     raw = raw_ref[...]
     unit = images[PAIRS:2 * PAIRS, :].astype(F32)
     for late in range(2):
@@ -479,9 +485,6 @@
     feats_cross.wait_recv()
     for copy in parts:
         copy.wait_recv()
-
-    def rows(index):
-        return pl.ds(pl.multiple_of(index * PADDED, 16), PADDED)
 
     x_moves = []
     for o in (1, 2, 3, 0):
@@ -521,14 +524,18 @@
     grad = jnp.concatenate([upper, lower], axis=0)
 
     new_sum = state_tile[0] + grad
-    update = new_sum + state_tile[1]
+    update_all[rows(z), :] = new_sum + state_tile[1]
+    moves = [net.push(update_all.at[rows(z), :], update_all.at[rows(z), :], target) for target in at_z]
     for piece in range(8):
         first = 11 * (piece // 2) + 5 * (piece % 2)
         sums_send[piece] = new_sum[first:first + 8]
-
-    square = jnp.sum((update * update).reshape(PADDED // 8, 8, 128), axis=0)
+    arrive(start_moves)
+    arrive(moves)
+
+    update = update_all[...]
+    square = jnp.sum((update * update).reshape(WIDE // 8, 8, 128), axis=0)
     at = 0
-    for stage, targets in enumerate((at_z, at_x, at_y + [across] + at_y_across)):
+    for stage, targets in enumerate((at_x, at_y + [across] + at_y_across)):
         sq_send[stage] = square
         moves = [
             net.push(sq_send.at[stage], sq_recv.at[at + i], target)
@@ -541,38 +548,31 @@
     norm = jnp.sqrt(jnp.sum(square, keepdims=True))
     cap = math.sqrt(W * E)
     shrink = cap / jnp.maximum(norm, cap)
-    tile = (state_tile[2] - RATE * shrink * update).astype(BF16)
-
-    z_tiles[rows(z), :] = tile
-    moves = [net.push(z_tiles.at[rows(z), :], z_tiles.at[rows(z), :], target) for target in at_z]
+
+    whole = start_all[...] - RATE * shrink * update
+    whole = jnp.concatenate([whole[piece * PADDED:piece * PADDED + BLOCK] for piece in range(Z)], axis=0)
+    weights_ref[x, :, lanes(k)] = whole.astype(BF16)
+
+    half = SHARE // 2
+
+    def low_piece(index, rows=(0, half)):
+        return weights_ref.at[index, rows[0]:rows[1], lanes(c, 512)]
+
+    def high_piece(away, shares=slice(0, X)):
+        return weights_ref.at[shares, half:SHARE, lanes(c * 4 + shift(y, away, Y))]
+
+    def send(piece, target):
+        return net.push(piece, piece, target)
+
+    moves_y = [send(weights_ref.at[x, 0:half, lanes(k)], target) for target in at_y]
+    moves_x = [send(weights_ref.at[x, half:SHARE, lanes(k)], target) for target in at_x]
     sums_out = Scatter(
         net, sums_send, sums_ref,
         [device(x, 2 * zl + i // 4, zh2 + (i // 2) % 2, i % 2) for i in range(8)],
-        [
-            jnp.logical_and(half_y == zl, owner_slot == i) for i in range(8)
-        ],
+        [jnp.logical_and(half_y == zl, owner_slot == i) for i in range(8)],
         k,
     )
     sums_out.start()
-    for copy in moves:
-        copy.wait_recv()
-    whole = z_tiles[...].astype(F32)
-    whole = jnp.concatenate([whole[piece * PADDED:piece * PADDED + BLOCK] for piece in range(Z)], axis=0)
-    weights_ref[x, :, lanes(k)] = whole.astype(BF16)
-
-    half = SHARE // 2
-
-    def low_piece(index, rows=(0, half)):
-        return weights_ref.at[index, rows[0]:rows[1], lanes(c, 512)]
-
-    def high_piece(away, shares=slice(0, X)):
-        return weights_ref.at[shares, half:SHARE, lanes(c * 4 + shift(y, away, Y))]
-
-    def send(piece, target):
-        return net.push(piece, piece, target)
-
-    moves_y = [send(weights_ref.at[x, 0:half, lanes(k)], target) for target in at_y]
-    moves_x = [send(weights_ref.at[x, half:SHARE, lanes(k)], target) for target in at_x]
     arrive(moves_y)
     low_moves = [send(low_piece(x), target) for target in (x_up, x_down)]
     arrive(moves_x)
@@ -608,7 +608,9 @@
     state = jnp.pad(jnp.stack([grad_sum, tree_noise, init_weights]), ((0, 0), (4, 4), (0, 0)))
     state = lax.dynamic_slice(state, (0, 4 - 4 * c, 0), (3, 48, 128))
     state = state.reshape(3, 6, 8, 128).transpose(2, 0, 1, 3)
-    state = jnp.pad(state, ((0, 0), (0, 0), (0, 2), (0, 0)))
+    users = jnp.stack([user_ids.astype(F32), jnp.pad(clip_norms, (0, PAIRS - USERS))])
+    users = jnp.pad(users[None, None], ((0, 7), (0, 2), (0, 0), (0, 0)))
+    state = jnp.concatenate([state, users], axis=2)
     vmem = pl.BlockSpec(memory_space=pltpu.VMEM)
     weights, sums = pl.pallas_call(
         kernel,
@@ -616,13 +618,11 @@
             jax.ShapeDtypeStruct((X, SHARE, E), BF16),
             jax.ShapeDtypeStruct((8, 8, 128), F32),
         ),
-        in_specs=[pl.BlockSpec(memory_space=pltpu.HBM)] * 6,
+        in_specs=[pl.BlockSpec(memory_space=pltpu.HBM)] * 4,
         out_specs=(vmem, vmem),
         scratch_shapes=[
             pltpu.VMEM((PAIRS, W), BF16),
             pltpu.VMEM((PAIRS, E), BF16),
-            pltpu.VMEM((1, USERS), F32),
-            pltpu.VMEM((1, PAIRS), jnp.int32),
             pltpu.VMEM((8, 3, 8, 128), F32),
             pltpu.VMEM((W, E), BF16),
             pltpu.VMEM((TEXTS, E), BF16),
@@ -652,13 +652,14 @@
             pltpu.VMEM((Z - 1, X, 16, 128), BF16),
             pltpu.VMEM((X, 16, 128), BF16),
             pltpu.VMEM((X - 1, 16, 128), BF16),
-            pltpu.VMEM((WIDE, 128), BF16),
+            pltpu.VMEM((WIDE, 128), F32),
+            pltpu.VMEM((WIDE, 128), F32),
             pltpu.VMEM((8, 3, 8, 128), F32),
             pltpu.VMEM((3, PADDED, 128), F32),
             pltpu.VMEM((8, 8, 128), F32),
             pltpu.VMEM((3, 8, 128), F32),
             pltpu.VMEM((17, 8, 128), F32),
-            pltpu.SemaphoreType.DMA((6,)),
+            pltpu.SemaphoreType.DMA((4,)),
             pltpu.SemaphoreType.DMA((COPIES,)),
             pltpu.SemaphoreType.DMA((COPIES,)),
         ],
@@ -666,8 +667,7 @@
             collective_id=1, has_side_effects=True, vmem_limit_bytes=48 * 1024 * 1024
         ),
     )(
-        image_feats, text_emb, projection, clip_norms.reshape(1, USERS),
-        user_ids.reshape(1, PAIRS), state,
+        image_feats, text_emb, projection, state,
     )
     sums = sums[:, :6].transpose(1, 0, 2).reshape(48, 128)
     return weights.reshape(W, E), lax.dynamic_slice(sums, (4 * c, 0), (44, 128))

time: 135 us -> 134 us (level)
    unnamed x9 -> x5, local copies, waits for them, and re-layouts: 4.82 us -> 3.51 us
where the time goes in v10:
time: 134 us
  Pallas kernels  127 us (95%)
  local copies, waits for them, and re-layouts  4.82 us (4%)
  other arithmetic  1.49 us (1%)
    pallas_call x1, Pallas kernels, body(): pl.pallas_call(kernel, out_shape=(jax.ShapeDtypeStruct((X, SHARE, E), BF1...  127 us
    unnamed x5, local copies, waits for them, and re-layouts  3.51 us

profile of v10, /device:TPU:1, one launch (start us, length us, event | category | flops | bytes accessed | tf_op | source)
XLA Modules:
  0.0 133.7 jit_solution(8363661342062421628)
XLA Ops:
  0.6 0.7 pad_bitcast_fusion
  1.3 0.7 convert_bitcast_fusion
  2.0 0.8 fusion.3
  2.8 0.0 copy-start
  2.8 1.0 copy-done
  3.8 0.0 copy-start.1
  3.8 0.9 copy-done.1
  4.8 126.7 %shard_map.95 = (bf16[4,352,1024]{2,1,0:T(8,128)(2,1)S(1)}, f32[8,8,128]{2,1,0:T(8,128)S(1)}) custom-call(bf16[128,1408]{1,0:T(8,128)(2,1)S(1)} %copy-done, bf16[128,1024]{1,0:T(8,128)(2,1)S(1)} %copy-done.1, bf16[1408,1024]{1,0:T(8,128)(2,1)} %proj_hbm.1, f32[8,3,8,128]{3,2,1,0:T(8,128)S(1)} %select_maximum_fusion.state_hbm), custom_call_target="tpu_custom_call" | custom-call | tf_op jit(solution)/shard_map/pallas_call | solution.py:615
  131.5 0.6 constant_dynamic-slice_fusion
  132.1 1.6 %copy.17 = bf16[1408,1024]{1,0:T(8,128)(2,1)} copy(bf16[1408,1024]{1,0:T(8,128)(2,1)S(1)} %bitcast.20) | data formatting | bytes 5767168
  (5 shorter events, 0.1 us)
Async XLA Ops:
  2.8 1.0 copy-start
  3.8 0.9 copy-start.1

commit v11 on v10

--- a/solution.py
+++ b/solution.py
@@ -428,9 +428,8 @@
         grid_step(pl.ds(pl.multiple_of(step * IMAGES, IMAGES), IMAGES), IMAGES, events)
         return carry
 
-    grid_step(slice(PAIRS, 2 * PAIRS), PAIRS, open_events)
     turn(3, 0)
-    grid_step(slice(0, PAIRS), PAIRS, lambda n: None)
+    grid_step(slice(0, IMAGES), IMAGES, open_events)
     give(0, 1)
     lax.fori_loop(1, 4, pair_step, 0)
     give(3, 0)

time: 134 us -> 131 us (0.978)
  Pallas kernels: 127 us -> 124 us
    pallas_call x1, Pallas kernels: 127 us -> 124 us  [body(): pl.pallas_call(kernel, out_shape=(jax.ShapeDtypeStruct((X, SHARE, E), BF1...]
where the time goes in v11:
time: 131 us
  Pallas kernels  124 us (95%)
  local copies, waits for them, and re-layouts  4.82 us (4%)
  other arithmetic  1.49 us (1%)
    pallas_call x1, Pallas kernels, body(): pl.pallas_call(kernel, out_shape=(jax.ShapeDtypeStruct((X, SHARE, E), BF1...  124 us
    unnamed x5, local copies, waits for them, and re-layouts  3.51 us

profile of v11, /device:TPU:1, one launch (start us, length us, event | category | flops | bytes accessed | tf_op | source)
XLA Modules:
  0.0 130.9 jit_solution(759686546271926236)
XLA Ops:
  0.6 0.7 pad_bitcast_fusion
  1.3 0.7 convert_bitcast_fusion
  2.0 0.8 fusion.3
  2.8 0.0 copy-start
  2.8 1.0 copy-done
  3.8 0.0 copy-start.1
  3.8 0.9 copy-done.1
  4.8 123.9 %shard_map.95 = (bf16[4,352,1024]{2,1,0:T(8,128)(2,1)S(1)}, f32[8,8,128]{2,1,0:T(8,128)S(1)}) custom-call(bf16[128,1408]{1,0:T(8,128)(2,1)S(1)} %copy-done, bf16[128,1024]{1,0:T(8,128)(2,1)S(1)} %copy-done.1, bf16[1408,1024]{1,0:T(8,128)(2,1)} %proj_hbm.1, f32[8,3,8,128]{3,2,1,0:T(8,128)S(1)} %select_maximum_fusion.state_hbm), custom_call_target="tpu_custom_call" | custom-call | tf_op jit(solution)/shard_map/pallas_call | solution.py:614
  128.7 0.6 constant_dynamic-slice_fusion
  129.3 1.6 %copy.17 = bf16[1408,1024]{1,0:T(8,128)(2,1)} copy(bf16[1408,1024]{1,0:T(8,128)(2,1)S(1)} %bitcast.20) | data formatting | bytes 5767168
  (5 shorter events, 0.1 us)
Async XLA Ops:
  2.8 1.0 copy-start
  3.8 0.9 copy-start.1

commit v12 on v11

--- a/solution.py
+++ b/solution.py
@@ -408,30 +408,24 @@
         if n == 2:
             arrive(text_crossings)
 
-    schedule = {
-        (2, 0): [lambda: give(1, 0), lambda: give(1, 1)],
-        (2, 1): [feats_on],
-        (3, 0): [lambda: give(2, 0)],
-        (3, 2): [lambda: give(2, 1), feats_over],
-    }
-
-    def pair_step(step, carry):
-        def events(n):
-            for (at, part), todo in schedule.items():
-                if part == n:
-
-                    @pl.when(step == at)
-                    def _(todo=todo):
-                        for event in todo:
-                            event()
-
-        grid_step(pl.ds(pl.multiple_of(step * IMAGES, IMAGES), IMAGES), IMAGES, events)
-        return carry
+    def middle_events(n):
+        if n == 2:
+            feats_on()
+
+    def last_events(n):
+        if n == 2:
+            give(2, 0)
+            feats_over()
+        if n == 3:
+            give(2, 1)
 
     turn(3, 0)
     grid_step(slice(0, IMAGES), IMAGES, open_events)
     give(0, 1)
-    lax.fori_loop(1, 4, pair_step, 0)
+    grid_step(slice(IMAGES, 3 * IMAGES), 2 * IMAGES, middle_events)
+    give(1, 0)
+    give(1, 1)
+    grid_step(slice(3 * IMAGES, 4 * IMAGES), IMAGES, last_events)
     give(3, 0)
     give(3, 1)
     unit = images[PAIRS:2 * PAIRS, :].astype(F32)
@@ -629,8 +623,8 @@
             pltpu.VMEM((PAIRS, E), F32),
             pltpu.VMEM((Z * PAIRS, E), F32),
             pltpu.VMEM((PAIRS, E), F32),
-            pltpu.VMEM((IMAGES, CHUNK), BF16),
-            pltpu.VMEM((IMAGES, CHUNK), BF16),
+            pltpu.VMEM((2 * IMAGES, CHUNK), BF16),
+            pltpu.VMEM((2 * IMAGES, CHUNK), BF16),
             pltpu.VMEM((7, HALF, E), BF16),
             pltpu.VMEM((7, HALF, E), BF16),
             pltpu.VMEM((7, HALF, E), BF16),

time: 131 us -> 133 us (1.015)
  Pallas kernels: 124 us -> 126 us
    pallas_call x1, Pallas kernels: 124 us -> 126 us  [body(): pl.pallas_call(kernel, out_shape=(jax.ShapeDtypeStruct((X, SHARE, E), BF1...]
where the time goes in v12:
time: 133 us
  Pallas kernels  126 us (95%)
  local copies, waits for them, and re-layouts  4.82 us (4%)
  other arithmetic  1.49 us (1%)
    pallas_call x1, Pallas kernels, body(): pl.pallas_call(kernel, out_shape=(jax.ShapeDtypeStruct((X, SHARE, E), BF1...  126 us
    unnamed x5, local copies, waits for them, and re-layouts  3.51 us

profile of v12, /device:TPU:1, one launch (start us, length us, event | category | flops | bytes accessed | tf_op | source)
XLA Modules:
  0.0 133.0 jit_solution(16418885229216390537)
XLA Ops:
  0.6 0.7 pad_bitcast_fusion
  1.3 0.7 convert_bitcast_fusion
  2.0 0.8 fusion.3
  2.8 0.0 copy-start
  2.8 1.0 copy-done
  3.8 0.0 copy-start.1
  3.8 0.9 copy-done.1
  4.8 126.0 %shard_map.95 = (bf16[4,352,1024]{2,1,0:T(8,128)(2,1)S(1)}, f32[8,8,128]{2,1,0:T(8,128)S(1)}) custom-call(bf16[128,1408]{1,0:T(8,128)(2,1)S(1)} %copy-done, bf16[128,1024]{1,0:T(8,128)(2,1)S(1)} %copy-done.1, bf16[1408,1024]{1,0:T(8,128)(2,1)} %proj_hbm.1, f32[8,3,8,128]{3,2,1,0:T(8,128)S(1)} %select_maximum_fusion.state_hbm), custom_call_target="tpu_custom_call" | custom-call | tf_op jit(solution)/shard_map/pallas_call | solution.py:608
  130.8 0.6 constant_dynamic-slice_fusion
  131.4 1.6 %copy.17 = bf16[1408,1024]{1,0:T(8,128)(2,1)} copy(bf16[1408,1024]{1,0:T(8,128)(2,1)S(1)} %bitcast.20) | data formatting | bytes 5767168
  (5 shorter events, 0.1 us)
Async XLA Ops:
  2.8 1.0 copy-start
  3.8 0.9 copy-start.1
